TPU v7x, 256 devices: a whole 4x4x8 slice. The times are simulated.
256 devices in a mesh: section: 16 (over z, core), tensor: 8 (over y_hi, x), group: 2 (over y_lo).
Axes of the slice: x: 4, y: 4 (y_hi: 2, y_lo: 2; y = y_hi * 2 + y_lo), z: 8, core: 2. Of those that a mesh axis runs over, the one named last changes fastest.
Arguments:
- layer_deltas: bfloat16 [32, 256, 16384], P('section', 'group', 'tensor'), may hold values from -6 to 6
- tap_layers: int32 [3], replicated, may hold values from 0 to 31, as said below
- norm_gain: float32 [3, 16384], P(None, 'tensor'), may hold values from 0.1 to 1.9
- fc_weight: bfloat16 [3, 16384, 16384], P(None, 'tensor', ('section', 'group')), may hold values from -0.02734375 to 0.02734375
Outputs:
- joined: bfloat16 [256, 16384], P(None, ('section', 'group'))
Inputs may be any that keep to these rules, and one draw needn't show every extreme that they name: `tap_layers`: three layers, strictly rising: low in the first third of the 32 layers, mid in the second, high the last layer.
All inputs are finite; a program needn't handle non-finite values.
Results may differ from a plain program's by a relative error of at most 0.005.
Values may be sent and summed in bfloat16 or wider, within the bound.
No kernel may reach another device: no remote copies, remote signals or barrier semaphores. Data moves between devices by JAX's collectives and lax.ppermute only.
A program may use at most 64 MiB of HBM per device.

v0:
```python
import jax
import jax.numpy as jnp
from jax import lax
from jax.sharding import PartitionSpec as P

D = 16384


EPS = 1e-05


def prefix(shard, axis, combine, identity):
    count, position = (lax.axis_size(axis), lax.axis_index(axis))
    everything = lax.all_gather(shard, axis)
    start = jnp.broadcast_to(jnp.asarray(identity, shard.dtype), shard.shape)

    def hop(k, before):
        reached = k < position
        new = combine(before, everything[k])
        return jnp.where(reached, new, before)

    return lax.fori_loop(0, count, hop, start)


def broadcast(shard, axis, root):
    mine = lax.axis_index(axis) == root
    return lax.psum(jnp.where(mine, shard, jnp.zeros_like(shard)), axis)


def normalize(picks, gain):
    squares = jnp.sum(picks * picks, axis=2)
    totals = lax.psum(squares, "tensor")
    scale = lax.rsqrt(totals / D + EPS)
    return (picks * scale[:, :, None] * gain[:, None, :]).astype(jnp.bfloat16)


def join_rows(weights):

    def project(piece, start):
        total = jnp.dot(piece[0], weights[0], preferred_element_type=jnp.float32)
        total = total + jnp.dot(piece[1], weights[1], preferred_element_type=jnp.float32)
        return total + jnp.dot(piece[2], weights[2], preferred_element_type=jnp.float32)

    return project


def shards(layer_deltas, tap_layers, norm_gain, fc_weight):
    layers_here = layer_deltas.shape[0]
    first = lax.axis_index("section") * layers_here
    deltas = layer_deltas.astype(jnp.float32)
    project = join_rows(fc_weight)
    local = jnp.cumsum(deltas, axis=0)
    before = prefix(local[-1], "section", jnp.add, jnp.zeros_like(local[-1]))
    states = local + before[None]
    picks = []
    for which in range(3):
        slot = jnp.clip(tap_layers[which] - first, 0, layers_here - 1)
        picks.append(lax.dynamic_index_in_dim(states, slot, 0, keepdims=False))
    normed = normalize(jnp.stack(picks), norm_gain)
    shared = []
    for which in range(3):
        owner = tap_layers[which] // layers_here
        shared.append(broadcast(normed[which], "section", owner))
    shared = jnp.stack(shared)
    joined = project(lax.all_gather(shared, "group", axis=1, tiled=True), jnp.int32(0))
    total = lax.psum(joined, "tensor")
    return total.astype(jnp.bfloat16)


def solution(mesh):
    in_specs = (
        P("section", "group", "tensor"),
        P(),
        P(None, "tensor"),
        P(None, "tensor", ("section", "group")),
    )
    out_specs = P(None, ("section", "group"))
    return jax.shard_map(shards, mesh=mesh, in_specs=in_specs, out_specs=out_specs, check_vma=False)
```

profile of v0, /device:TPU:1, one launch (start us, length us, event | category | flops | bytes accessed | tf_op | source)
XLA Modules:
  0.0 376.4 jit_solution(9542049897829103725)
XLA Ops:
  6.5 0.0 copy-start.1
  6.5 0.0 all-gather.3.cloned.1.call-start
  6.5 1.4 fusion.9
  7.9 1.1 slice.55
  9.0 0.0 all-gather.3.cloned.1.call-update
  9.0 0.0 all-reduce.4.cloned.1.call-start
  9.1 0.0 copy-done.1
  9.1 0.7 fusion.17
  18.9 90.0 %all-gather.3.cloned.1.call-done = f32[16,128,2048]{2,1,0:T(8,128)} async-done(((f32[1,128,2048]{2,1,0:T(8,128)}), f32[16,128,2048]{2,1,0:T(8,128)}) %all-gather.3.cloned.1.call-update) | async-done | bytes 16777232 | tf_op jit(solution)/shard_map/all_gather | solution.py:14
  108.9 25.8 %while.14 = (s32[]{:T(128)}, f32[128,2048]{1,0:T(8,128)S(1)}, s32[]{:T(128)}, f32[16,128,2048]{2,1,0:T(8,128)}, s32[]{:T(128)}, /*index=5*/s32[]{:T(128)}) while((s32[]{:T(128)}, f32[128,2048]{1,0:T(8,128)S(1)}, s32[]{:T(128)}, f32[16,128,2048]{2,1,0:T(8,128)}, s32[]{:T(128)}, /*index=5*/s32[]{:T(128)}) %tuple.38), condition=%wide.region_2.3_spmd.clone, body=%wide.region_1.2_spmd.clone.sunk | while | flops 786436 | bytes 3145829 | solution.py:22
  108.9 1.6 add_select_fusion.2
  110.5 1.6 add_select_fusion.2
  112.1 1.6 add_select_fusion.2
  113.7 1.6 add_select_fusion.2
  115.3 1.6 add_select_fusion.2
  116.9 1.6 add_select_fusion.2
  118.5 1.6 add_select_fusion.2
  120.1 1.6 add_select_fusion.2
  121.8 1.6 add_select_fusion.2
  123.4 1.6 add_select_fusion.2
  125.0 1.6 add_select_fusion.2
  126.6 1.6 add_select_fusion.2
  128.2 1.6 add_select_fusion.2
  129.8 1.6 add_select_fusion.2
  131.4 1.6 add_select_fusion.2
  133.1 1.6 add_select_fusion.2
  134.7 0.2 broadcast_add_fusion
  134.9 0.2 constant_dynamic-slice_fusion.2
  135.1 0.0 copy-start
  135.1 0.3 multiply_reduce_fusion
  135.4 20.3 %psum.35 = f32[3,128]{1,0:T(4,128)S(1)} all-reduce(f32[3,128]{1,0:T(4,128)S(1)} %multiply_reduce_fusion), channel_id=1, replica_groups=mesh['section'=16,'tensor'=8,'group'=2] {'tensor'}, use_global_device_ids=true, to_apply=%region_4.5 | all-reduce | flops 384 | bytes 3072 | tf_op jit(solution)/shard_map/psum | solution.py:32
  155.7 0.0 copy-done
  155.7 0.3 multiply_convert_fusion
  156.1 1.2 slice_select_fusion.2
  157.3 0.0 all-reduce.4.cloned.1.call-update
  157.3 0.0 all-gather.5.cloned.1.call-start
  157.3 111.0 %all-reduce.4.cloned.1.call-done = (bf16[1,128,2048]{2,1,0:T(8,128)(2,1)}, bf16[1,128,2048]{2,1,0:T(8,128)(2,1)}, bf16[1,128,2048]{2,1,0:T(8,128)(2,1)}) async-done(((bf16[1,128,2048]{2,1,0:T(8,128)(2,1)}, bf16[1,128,2048]{2,1,0:T(8,128)(2,1)}, bf16[1,128,2048]{2,1,0:T(8,128)(2,1)}), (bf16[1,128,2048]{2,1,0:T(8,128)(2,1)}, bf16[1,128,2048]{2,1,0:T(8,128)(2,1)}, ...) | async-done | bytes 1572880 | tf_op jit(solution)/shard_map/psum | solution.py:27
  268.3 2.7 pad_maximum_fusion.1
  271.0 0.0 all-gather.5.cloned.1.call-update
  271.0 50.6 %all-gather.5.cloned.1.call-done = bf16[3,256,2048]{2,1,0:T(8,128)(2,1)} async-done(((bf16[3,128,2048]{2,1,0:T(8,128)(2,1)}), bf16[3,256,2048]{2,1,0:T(8,128)(2,1)}) %all-gather.5.cloned.1.call-update) | async-done | bytes 3145744 | tf_op jit(solution)/shard_map/all_gather | solution.py:65
  321.7 0.0 copy-start.2
  321.7 2.8 fusion
  324.4 0.1 copy-done.2
  324.5 2.3 fusion.2
  326.8 2.3 fusion.14
  329.2 40.7 %all-reduce.5 = bf16[256,512]{1,0:T(8,128)(2,1)} all-reduce(f32[256,512]{1,0:T(8,128)S(1)} %fusion.14), channel_id=1, replica_groups=mesh['section'=16,'tensor'=8,'group'=2] {'tensor'}, use_global_device_ids=true, to_apply=%region_8.9 | all-reduce | flops 131072 | bytes 786432 | tf_op jit(solution)/shard_map/psum | solution.py:66
  (2 shorter events, 0.0 us)
Async XLA Ops:
  6.5 2.5 copy-start.1
  6.5 102.3 %all-gather.3.cloned.1.call-start = ((), (), s32[]{:S(2)}) async-start(), calls=%async_computation | async-start | bytes 17825792 | tf_op jit(solution)/shard_map/all_gather | solution.py:14
  9.0 259.3 %all-reduce.4.cloned.1.call-start = ((), (), s32[]{:S(2)}) async-start(), calls=%async_computation.2 | async-start | bytes 3145728 | tf_op jit(solution)/shard_map/psum | solution.py:27
  135.1 20.6 %copy-start = (f32[3,2048]{1,0:T(4,128)S(1)}, f32[3,2048]{1,0:T(4,128)}, u32[]{:S(2)}) copy-start(f32[3,2048]{1,0:T(4,128)} %param.8) | copy-start | bytes 73732
  157.3 164.4 %all-gather.5.cloned.1.call-start = ((), (), s32[]{:S(2)}) async-start(), calls=%async_computation.1 | async-start | bytes 4718592 | tf_op jit(solution)/shard_map/all_gather | solution.py:65
  321.7 2.8 copy-start.2
Sparse Core Ops, SparseCore 0:
  9.2 99.6 all-gather.2
  157.4 110.8 all-reduce.3
  271.2 50.4 all-gather.4
where the time goes:
time: 383 us; the launch traced here: 376 us
  waiting for transfers between devices  252 us (66%)
  blocking collectives  61 us (16%)
  other arithmetic  31.5 us (8%)
  between operations  22.3 us (6%)
  matrix products  7.39 us (2%)
    psum x1, waiting for transfers between devices, broadcast(): return lax.psum(jnp.where(mine, shard, jnp.zeros_like(shard)), axis)  111 us
    all_gather x1, waiting for transfers between devices, prefix(): everything = lax.all_gather(shard, axis)  90 us
    all_gather x1, waiting for transfers between devices, shards(): lax.all_gather(shared, 'group', axis=1, tiled=True)  50.6 us
    psum x1, blocking collectives, shards(): total = lax.psum(joined, 'tensor')  40.7 us
    select_n x16, other arithmetic, hop(): return jnp.where(reached, new, before)  25.4 us
    psum x1, blocking collectives, normalize(): totals = lax.psum(squares, 'tensor')  20.3 us
  transfers between devices with their start and end apart: 3, of which 3 were waited for; matrix products, arithmetic and copies ran while one was open for 0% of the time, Pallas kernels for 0%

commit v1 on v0

v1 whole, which is shorter than its diff:
```python
import jax
import jax.numpy as jnp
from jax import lax
from jax.experimental import pallas as pl
from jax.experimental.pallas import tpu as pltpu
from jax.sharding import Mesh, PartitionSpec as P

D = 16384
EPS = 1e-05
Z, CORE, HI, X, LO = "z", "core", "hi", "x", "lo"
BF, F32 = jnp.bfloat16, jnp.float32
ROWS = 16
HALF = 1024
MIB = 1 << 20

VMEM = pl.BlockSpec(memory_space=pltpu.VMEM)
SMEM = pl.BlockSpec(memory_space=pltpu.SMEM)


def call(kernel, shape, specs, *args, flops=0, limit=32):
    size = sum(a.size * a.dtype.itemsize for a in args)
    return pl.pallas_call(
        kernel,
        out_shape=shape,
        in_specs=specs,
        out_specs=VMEM,
        cost_estimate=pl.CostEstimate(flops=flops, bytes_accessed=size, transcendentals=0),
        compiler_params=pltpu.CompilerParams(vmem_limit_bytes=limit * MIB),
    )(*args)


def half_of(core):
    return pl.ds(pl.multiple_of(core * HALF, HALF), HALF)


def segments(tap_ref, delta_ref, tokens, columns):
    first = (lax.axis_index(Z) * 2 + lax.axis_index(CORE)) * 2
    layers = [delta_ref[j, tokens, columns].astype(F32) for j in range(2)]
    out = []
    for k in range(3):
        total = None
        for j in range(2):
            inside = first + j <= tap_ref[k]
            if k:
                inside = jnp.logical_and(inside, first + j > tap_ref[k - 1])
            term = layers[j] * jnp.where(inside, 1.0, 0.0).astype(F32)
            total = term if total is None else total + term
        out.append(total)
    return out


def send_kernel(tap_ref, delta_ref, out_ref):
    columns = half_of(1 - lax.axis_index(CORE))
    for piece in range(8):
        for k, part in enumerate(segments(tap_ref, delta_ref, pl.ds(piece * ROWS, ROWS), columns)):
            out_ref[piece, k] = part.astype(BF)


def pair_kernel(tap_ref, delta_ref, other_ref, out_ref):
    columns = half_of(lax.axis_index(CORE))
    for piece in range(8):
        for k, part in enumerate(segments(tap_ref, delta_ref, pl.ds(piece * ROWS, ROWS), columns)):
            out_ref[piece, k] = (part + other_ref[piece, k].astype(F32)).astype(BF)


def tapped_kernel(parts_ref, gain_ref, out_ref):
    columns = half_of(lax.axis_index(CORE))
    state = None
    for k in range(3):
        total = parts_ref[0, k].astype(F32)
        for piece in range(1, 8):
            total = total + parts_ref[piece, k].astype(F32)
        state = total if state is None else state + total
        scaled = (state * gain_ref[pl.ds(k, 1), columns]).astype(BF)
        for copy in range(out_ref.shape[0]):
            out_ref[copy, k] = scaled


def join_kernel(mine_ref, other_ref, weight_ref, gain_ref, out_ref):
    core = lax.axis_index(CORE)
    lane = lax.broadcasted_iota(jnp.int32, (16, 512), 1) // 64
    squares = [[None] * 3 for _ in range(16)]
    for k in range(3):
        total = None
        sums = None
        for ref, side in ((mine_ref, core), (other_ref, 1 - core)):
            states = ref[:, k].reshape(256, HALF)
            weights = weight_ref[k, half_of(side), :]
            product = jnp.dot(states, weights, preferred_element_type=F32)
            plain = states.astype(F32) / gain_ref[pl.ds(k, 1), half_of(side)]
            square = jnp.sum(plain * plain, axis=1, keepdims=True)
            total = product if total is None else total + product
            sums = square if sums is None else sums + square
        out_ref[:, k * 32 : (k + 1) * 32, :] = total.reshape(8, 32, 512).astype(BF)
        for block in range(16):
            squares[block][k] = sums[block * 16 : (block + 1) * 16]
    for piece in range(8):
        packed = jnp.zeros((16, 512), F32)
        for h in range(2):
            for k in range(3):
                packed = jnp.where(lane == 2 * k + h, squares[2 * piece + h][k], packed)
        out_ref[piece, 96:112, :] = packed.astype(BF)


def scale_kernel(parts_ref, out_ref):
    squares = parts_ref[0, 96:112, :].astype(F32)
    for piece in range(1, 8):
        squares = squares + parts_ref[piece, 96:112, :].astype(F32)
    scale = lax.rsqrt(squares / D + EPS)
    for h in range(2):
        joined = None
        for k in range(3):
            rows = pl.ds(k * 32 + h * 16, 16)
            total = parts_ref[0, rows, :].astype(F32)
            for piece in range(1, 8):
                total = total + parts_ref[piece, rows, :].astype(F32)
            at = 64 * (2 * k + h)
            total = total * scale[:, at : at + 1]
            joined = total if joined is None else joined + total
        joined = joined.astype(BF)
        for copy in range(8):
            out_ref[copy, h * 16 : (h + 1) * 16, :] = joined


def swap(a, axis):
    return lax.ppermute(a, axis, [(0, 1), (1, 0)])


def exchange(a, axes):
    return lax.all_to_all(a, axes, 0, 0, tiled=True)


def shards(layer_deltas, tap_layers, norm_gain, fc_weight):
    pieces = jax.ShapeDtypeStruct((8, 3, ROWS, HALF), BF)
    sent = call(send_kernel, pieces, [SMEM, VMEM], tap_layers, layer_deltas)
    other = swap(sent, CORE)
    paired = call(pair_kernel, pieces, [SMEM, VMEM, VMEM], tap_layers, layer_deltas, other)
    parts = exchange(paired, (Z,))
    copies = jax.ShapeDtypeStruct((16, 3, ROWS, HALF), BF)
    mine = call(tapped_kernel, copies, [VMEM, VMEM], parts, norm_gain)
    mine = exchange(mine, (LO, Z))
    other = swap(mine, CORE)
    partial = jax.ShapeDtypeStruct((8, 112, 512), BF)
    partial = call(
        join_kernel, partial, [VMEM] * 4, mine, other, fc_weight, norm_gain, flops=2 * 256 * 6144 * 512
    )
    partial = exchange(partial, (HI, X))
    joined = call(scale_kernel, jax.ShapeDtypeStruct((8, 32, 512), BF), [VMEM], partial)
    return exchange(joined, (HI, X)).reshape(256, 512)


def solution(mesh):
    fine = Mesh(mesh.devices.reshape(8, 2, 2, 4, 2), (Z, CORE, HI, X, LO))
    in_specs = (P((Z, CORE), LO, (HI, X)), P(), P(None, (HI, X)), P(None, (HI, X), (Z, CORE, LO)))
    out_specs = P(None, (Z, CORE, LO))
    return jax.shard_map(shards, mesh=fine, in_specs=in_specs, out_specs=out_specs, check_vma=False)
```

time: 383 us -> 118 us (0.31); the launches traced: 376 us -> 117 us
  waiting for transfers between devices: 252 us -> 4.95 us
  blocking collectives: 61 us -> 99.3 us
  other arithmetic: 31.5 us -> 0 us
  between operations: 22.3 us -> 0.06 us
  matrix products: 7.39 us -> 0 us
  starting transfers between devices: 0.09 us -> 6.42 us
  Pallas kernels: 0 us -> 4.11 us
    all_gather x2 -> x0, waiting for transfers between devices: 141 us -> none  [the longest x1 90 us: prefix(): everything = lax.all_gather(shard, axis)]
    psum x1 -> x0, waiting for transfers between devices: 111 us -> none  [broadcast(): return lax.psum(jnp.where(mine, shard, jnp.zeros_like(shard)), axis)]
    all_to_all x0 -> x4, blocking collectives: none -> 99.3 us  [exchange(): return lax.all_to_all(a, axes, 0, 0, tiled=True)]
    psum x2 -> x0, blocking collectives: 61 us -> none  [the longest x1 40.7 us: shards(): total = lax.psum(joined, 'tensor')]
    select_n x17 -> x0, other arithmetic: 26.6 us -> none  [the longest x16 25.4 us: hop(): return jnp.where(reached, new, before)]
    dot_general x3 -> x0, matrix products: 7.39 us -> none  [the longest x1 2.75 us: project(): jnp.dot(piece[2], weights[2], preferred_element_type=jnp.float32)]
    ppermute x0 -> x2, starting transfers between devices: none -> 6.42 us  [swap(): return lax.ppermute(a, axis, [(0, 1), (1, 0)])]
    ppermute x0 -> x2, waiting for transfers between devices: none -> 4.95 us  [swap(): return lax.ppermute(a, axis, [(0, 1), (1, 0)])]
  transfers between devices with their start and end apart: 3 -> 2, of which waited for: 3 -> 2; matrix products, arithmetic and copies ran while one was open for 0% -> 0% of each run, Pallas kernels for 0% -> 0%
where the time goes in v1:
time: 118 us; the launch traced here: 117 us
  blocking collectives  99.3 us (84%)
  starting transfers between devices  6.42 us (5%)
  waiting for transfers between devices  4.95 us (4%)
  Pallas kernels  4.11 us (3%)
  local copies, waits for them, and re-layouts  2.59 us (2%)
    all_to_all x4, blocking collectives, exchange(): return lax.all_to_all(a, axes, 0, 0, tiled=True)  99.3 us
    ppermute x2, starting transfers between devices, swap(): return lax.ppermute(a, axis, [(0, 1), (1, 0)])  6.42 us
    ppermute x2, waiting for transfers between devices, swap(): return lax.ppermute(a, axis, [(0, 1), (1, 0)])  4.95 us
    pallas_call x5, Pallas kernels, call(): pl.pallas_call(kernel, out_shape=shape, in_specs=specs, out_specs=VMEM, c...  4.11 us
    unnamed x9, local copies, waits for them, and re-layouts  2.59 us
  transfers between devices with their start and end apart: 2, of which 2 were waited for; matrix products, arithmetic and copies ran while one was open for 0% of the time, Pallas kernels for 0%

profile of v1, /device:TPU:1, one launch (start us, length us, event | category | flops | bytes accessed | tf_op | source)
XLA Modules:
  0.0 117.5 jit_solution(15976397083861164830)
XLA Ops:
  0.0 0.0 copy-start.1
  0.0 1.2 %copy-done.1 = bf16[2,128,2048]{2,1,0:T(8,128)(2,1)S(1)} copy-done((bf16[2,128,2048]{2,1,0:T(8,128)(2,1)S(1)}, bf16[2,128,2048]{2,1,0:T(8,128)(2,1)}, u32[]{:S(2)}) %copy-start.1) | copy-done | bytes 1048600
  1.2 0.0 copy-start.3
  1.2 0.7 copy-done.3
  1.9 0.8 shard_map.46
  2.7 0.0 copy-start.2
  2.7 3.3 %collective-permute-start = (bf16[8,3,16,1024]{3,2,1,0:T(8,128)(2,1)S(1)}, bf16[8,3,16,1024]{3,2,1,0:T(8,128)(2,1)S(1)}, u32[]{:S(2)}, u32[]{:S(2)}) collective-permute-start(bf16[8,3,16,1024]{3,2,1,0:T(8,128)(2,1)S(1)} %shard_map.46), channel_id=1, source_target_pairs={{0,16},{16,0},{1,17},{17,1},{2,18},{18,2},{3,19},{19,3},{4,20},{20... | collective-permute-start | bytes 2359304 | tf_op jit(solution)/shard_map/ppermute | solution.py:126
  6.0 1.9 %collective-permute-done.other_ref = bf16[8,3,16,1024]{3,2,1,0:T(8,128)(2,1)S(1)} collective-permute-done((bf16[8,3,16,1024]{3,2,1,0:T(8,128)(2,1)S(1)}, bf16[8,3,16,1024]{3,2,1,0:T(8,128)(2,1)S(1)}, u32[]{:S(2)}, u32[]{:S(2)}) %collective-permute-start) | collective-permute-done | bytes 786464 | tf_op jit(solution)/shard_map/ppermute | solution.py:126
  7.9 0.9 shard_map.47
  8.8 0.0 copy-start
  8.8 28.8 %all_to_all.20.parts_ref = bf16[8,3,16,1024]{3,2,1,0:T(8,128)(2,1)S(1)} all-to-all(bf16[8,3,16,1024]{3,2,1,0:T(8,128)(2,1)S(1)} %shard_map.47), channel_id=1, replica_groups=mesh['z'=8,'core'=2,'hi'=2,'x'=4,'lo'=2] {'z'}, dimensions={0} | all-to-all | bytes 1572864 | tf_op jit(solution)/shard_map/all_to_all | solution.py:130
  37.6 0.0 copy-done.2
  37.6 0.2 shard_map.48
  37.8 38.3 %all_to_all.21.mine_ref = bf16[16,3,16,1024]{3,2,1,0:T(8,128)(2,1)S(1)} all-to-all(bf16[16,3,16,1024]{3,2,1,0:T(8,128)(2,1)S(1)} %shard_map.48), channel_id=1, replica_groups=mesh['z'=8,'core'=2,'hi'=2,'x'=4,'lo'=2] {'lo','z'}, dimensions={0} | all-to-all | bytes 3145728 | tf_op jit(solution)/shard_map/all_to_all | solution.py:130
  76.1 3.1 %collective-permute-start.1 = (bf16[16,3,16,1024]{3,2,1,0:T(8,128)(2,1)S(1)}, bf16[16,3,16,1024]{3,2,1,0:T(8,128)(2,1)S(1)}, u32[]{:S(2)}, u32[]{:S(2)}) collective-permute-start(bf16[16,3,16,1024]{3,2,1,0:T(8,128)(2,1)S(1)} %all_to_all.21.mine_ref), channel_id=1, source_target_pairs={{0,16},{16,0},{1,17},{17,1},{2,18},{18,2},{3,19},{19,3},{4,20},{20... | collective-permute-start | bytes 4718600 | tf_op jit(solution)/shard_map/ppermute | solution.py:126
  79.2 3.0 %collective-permute-done.1.other_ref = bf16[16,3,16,1024]{3,2,1,0:T(8,128)(2,1)S(1)} collective-permute-done((bf16[16,3,16,1024]{3,2,1,0:T(8,128)(2,1)S(1)}, bf16[16,3,16,1024]{3,2,1,0:T(8,128)(2,1)S(1)}, u32[]{:S(2)}, u32[]{:S(2)}) %collective-permute-start.1) | collective-permute-done | bytes 1572896 | tf_op jit(solution)/shard_map/ppermute | solution.py:126
  82.3 0.0 copy-done
  82.3 2.2 %shard_map.49 = bf16[8,112,512]{2,1,0:T(8,128)(2,1)S(1)} custom-call(bf16[16,3,16,1024]{3,2,1,0:T(8,128)(2,1)S(1)} %all_to_all.21.mine_ref, bf16[16,3,16,1024]{3,2,1,0:T(8,128)(2,1)S(1)} %collective-permute-done.1.other_ref, bf16[3,2048,512]{2,1,0:T(8,128)(2,1)S(1)} %copy-done, f32[3,2048]{1,0:T(4,128)S(1)} %copy-done.2), custom_call_target="tpu_custom_call" | custom-call | flops 1610612736 | bytes 9461760 | tf_op jit(solution)/shard_map/pallas_call | solution.py:22
  84.5 21.8 %all_to_all.22.parts_ref = bf16[8,112,512]{2,1,0:T(8,128)(2,1)S(1)} all-to-all(bf16[8,112,512]{2,1,0:T(8,128)(2,1)S(1)} %shard_map.49), channel_id=1, replica_groups=mesh['z'=8,'core'=2,'hi'=2,'x'=4,'lo'=2] {'hi','x'}, dimensions={0} | all-to-all | bytes 1835008 | tf_op jit(solution)/shard_map/all_to_all | solution.py:130
  106.2 0.1 shard_map.50
  106.4 10.4 %all_to_all.23 = bf16[8,32,512]{2,1,0:T(8,128)(2,1)S(1)} all-to-all(bf16[8,32,512]{2,1,0:T(8,128)(2,1)S(1)} %shard_map.50), channel_id=1, replica_groups=mesh['z'=8,'core'=2,'hi'=2,'x'=4,'lo'=2] {'hi','x'}, dimensions={0} | all-to-all | bytes 524288 | tf_op jit(solution)/shard_map/all_to_all | solution.py:130
  116.8 0.7 copy.6
Async XLA Ops:
  0.0 1.2 %copy-start.1 = (bf16[2,128,2048]{2,1,0:T(8,128)(2,1)S(1)}, bf16[2,128,2048]{2,1,0:T(8,128)(2,1)}, u32[]{:S(2)}) copy-start(bf16[2,128,2048]{2,1,0:T(8,128)(2,1)} %delta_ref.3) | copy-start | bytes 3145732
  1.2 0.7 copy-start.3
  2.7 35.0 %copy-start.2 = (f32[3,2048]{1,0:T(4,128)S(1)}, f32[3,2048]{1,0:T(4,128)}, u32[]{:S(2)}) copy-start(f32[3,2048]{1,0:T(4,128)} %gain_ref.3) | copy-start | bytes 73732
  2.7 5.2 %collective-permute-start = (bf16[8,3,16,1024]{3,2,1,0:T(8,128)(2,1)S(1)}, bf16[8,3,16,1024]{3,2,1,0:T(8,128)(2,1)S(1)}, u32[]{:S(2)}, u32[]{:S(2)}) collective-permute-start(bf16[8,3,16,1024]{3,2,1,0:T(8,128)(2,1)S(1)} %shard_map.46), channel_id=1, source_target_pairs={{0,16},{16,0},{1,17},{17,1},{2,18},{18,2},{3,19},{19,3},{4,20},{20... | collective-permute-start | bytes 2359304 | tf_op jit(solution)/shard_map/ppermute | solution.py:126
  8.8 73.5 %copy-start = (bf16[3,2048,512]{2,1,0:T(8,128)(2,1)S(1)}, bf16[3,2048,512]{2,1,0:T(8,128)(2,1)}, u32[]{:S(2)}) copy-start(bf16[3,2048,512]{2,1,0:T(8,128)(2,1)} %weight_ref.1) | copy-start | bytes 18874372
  76.1 6.1 %collective-permute-start.1 = (bf16[16,3,16,1024]{3,2,1,0:T(8,128)(2,1)S(1)}, bf16[16,3,16,1024]{3,2,1,0:T(8,128)(2,1)S(1)}, u32[]{:S(2)}, u32[]{:S(2)}) collective-permute-start(bf16[16,3,16,1024]{3,2,1,0:T(8,128)(2,1)S(1)} %all_to_all.21.mine_ref), channel_id=1, source_target_pairs={{0,16},{16,0},{1,17},{17,1},{2,18},{18,2},{3,19},{19,3},{4,20},{20... | collective-permute-start | bytes 4718600 | tf_op jit(solution)/shard_map/ppermute | solution.py:126

commit v2 on v1

v2 whole, which is shorter than its diff:
```python
import jax
import jax.numpy as jnp
from jax import lax
from jax.experimental import pallas as pl
from jax.experimental.pallas import tpu as pltpu
from jax.sharding import Mesh, PartitionSpec as P

D = 16384
EPS = 1e-05
ZQ, ZP, CORE, HI, X, LO = "zq", "zp", "core", "hi", "x", "lo"
Z = (ZQ, ZP)
BF, F32 = jnp.bfloat16, jnp.float32
ROWS = 16
HALF = 1024
MIB = 1 << 20

VMEM = pl.BlockSpec(memory_space=pltpu.VMEM)
SMEM = pl.BlockSpec(memory_space=pltpu.SMEM)
HBM = pl.BlockSpec(memory_space=pltpu.HBM)


def call(kernel, shapes, specs, *args, flops=0, limit=24, scratch=()):
    size = sum(a.size * a.dtype.itemsize for a in args)
    single = not isinstance(shapes, list)
    shapes = [shapes] if single else shapes
    out = pl.pallas_call(
        kernel,
        out_shape=[space(shape, kind) for shape, kind, space in shapes],
        in_specs=specs,
        out_specs=[pl.BlockSpec(memory_space=space) for _, _, space in shapes],
        scratch_shapes=list(scratch),
        cost_estimate=pl.CostEstimate(flops=flops, bytes_accessed=size, transcendentals=0),
        compiler_params=pltpu.CompilerParams(vmem_limit_bytes=limit * MIB),
    )(*args)
    return out[0] if single else out


def half_of(core):
    return pl.ds(pl.multiple_of(core * HALF, HALF), HALF)


def segments(tap_ref, delta_ref, tokens, columns):
    section = lax.axis_index(ZQ) * 4 + lax.axis_index(ZP) * 2 + lax.axis_index(CORE)
    first = section * 2
    layers = [delta_ref[j, tokens, columns].astype(F32) for j in range(2)]
    out = []
    for k in range(3):
        total = None
        for j in range(2):
            inside = first + j <= tap_ref[k]
            if k:
                inside = jnp.logical_and(inside, first + j > tap_ref[k - 1])
            term = layers[j] * jnp.where(inside, 1.0, 0.0).astype(F32)
            total = term if total is None else total + term
        out.append(total)
    return out


def send_kernel(tap_hbm, delta_hbm, gain_hbm, out_ref, tap_ref, delta_ref, gain_ref, sems):
    columns = half_of(1 - lax.axis_index(CORE))
    pairs = ((tap_hbm, tap_ref), (delta_hbm, delta_ref), (gain_hbm, gain_ref))
    copies = [pltpu.make_async_copy(a, b, sems.at[i]) for i, (a, b) in enumerate(pairs)]
    for copy in copies:
        copy.start()
    for copy in copies:
        copy.wait()
    for piece in range(8):
        for k, part in enumerate(segments(tap_ref, delta_ref, pl.ds(piece * ROWS, ROWS), columns)):
            out_ref[piece, k] = part.astype(BF)


def pair_kernel(tap_ref, delta_ref, other_ref, out_ref):
    columns = half_of(lax.axis_index(CORE))
    for piece in range(8):
        for k, part in enumerate(segments(tap_ref, delta_ref, pl.ds(piece * ROWS, ROWS), columns)):
            out_ref[piece, k] = (part + other_ref[piece, k].astype(F32)).astype(BF)


def tapped_kernel(parts_ref, gain_ref, out_ref):
    columns = half_of(lax.axis_index(CORE))
    state = None
    for k in range(3):
        total = parts_ref[0, k].astype(F32)
        for piece in range(1, 8):
            total = total + parts_ref[piece, k].astype(F32)
        state = total if state is None else state + total
        scaled = (state * gain_ref[pl.ds(k, 1), columns]).astype(BF)
        for copy in range(out_ref.shape[0]):
            out_ref[copy, k] = scaled


def blocks_of():
    zq, zp, lo = lax.axis_index(ZQ), lax.axis_index(ZP), lax.axis_index(LO)
    half = lax.rem(zq, 2)
    left = lax.rem(zq + zp + 1, 2)
    mine, yours, here, there = lo * 8, 8 - lo * 8, zp, 1 - zp
    out = [mine + 2 * i + here for i in range(4)]
    out += [mine + 2 * i + there for i in range(4)]
    out += [yours + 2 * (2 * half + i) + here for i in range(2)]
    out += [yours + 2 * (2 * left + i) + there for i in range(2)]
    out += [yours + 2 * (2 - 2 * left + i) + there for i in range(2)]
    out += [yours + 2 * (2 - 2 * half + i) + here for i in range(2)]
    return out


def cut_kernel(same_ref, left_ref, right_ref, early_ref, late_ref):
    at = 2 * lax.rem(lax.axis_index(ZQ), 2)
    left_ref[...] = same_ref[:2]
    right_ref[...] = same_ref[2:]
    early_ref[...] = same_ref[pl.ds(at, 2)]
    late_ref[...] = same_ref[pl.ds(2 - at, 2)]


def pack_kernel(*refs):
    for i, ref in enumerate(refs[:-1]):
        refs[-1][2 * i : 2 * i + 2] = ref[...]


def join_kernel(*refs):
    mine_refs, other_refs, (weight_ref, gain_ref, out_ref, state_ref) = refs[:3], refs[3:6], refs[6:]
    core = lax.axis_index(CORE)
    blocks = blocks_of()
    lane = lax.broadcasted_iota(jnp.int32, (16, 512), 1) // 64
    squares = [[None] * 3 for _ in range(16)]
    for k in range(3):
        total = None
        sums = None
        for side_refs, side in ((mine_refs, core), (other_refs, 1 - core)):
            at = 0
            for ref in side_refs:
                rows = ref.shape[0] * ROWS
                state_ref[at : at + rows, :] = ref[:, k].reshape(rows, HALF)
                at += rows
            states = state_ref[...]
            weights = weight_ref[k, half_of(side), :]
            product = jnp.dot(states, weights, preferred_element_type=F32)
            plain = states.astype(F32) / gain_ref[pl.ds(k, 1), half_of(side)]
            square = jnp.sum(plain * plain, axis=1, keepdims=True)
            total = product if total is None else total + product
            sums = square if sums is None else sums + square
        total = total.astype(BF)
        for i in range(16):
            rows = slice(i * ROWS, (i + 1) * ROWS)
            at = pl.multiple_of(k * 32 + lax.rem(blocks[i], 2) * 16, 16)
            out_ref[blocks[i] // 2, pl.ds(at, 16), :] = total[rows]
            squares[i][k] = sums[rows]
    out_ref[:, 96:112, :] = jnp.zeros((8, 16, 512), BF)
    for i in range(16):
        packed = out_ref[blocks[i] // 2, 96:112, :].astype(F32)
        for k in range(3):
            packed = jnp.where(lane == 2 * k + lax.rem(blocks[i], 2), squares[i][k], packed)
        out_ref[blocks[i] // 2, 96:112, :] = packed.astype(BF)


def scale_kernel(parts_ref, out_ref):
    squares = parts_ref[0, 96:112, :].astype(F32)
    for piece in range(1, 8):
        squares = squares + parts_ref[piece, 96:112, :].astype(F32)
    scale = lax.rsqrt(squares / D + EPS)
    for h in range(2):
        joined = None
        for k in range(3):
            rows = pl.ds(k * 32 + h * 16, 16)
            total = parts_ref[0, rows, :].astype(F32)
            for piece in range(1, 8):
                total = total + parts_ref[piece, rows, :].astype(F32)
            at = 64 * (2 * k + h)
            total = total * scale[:, at : at + 1]
            joined = total if joined is None else joined + total
        joined = joined.astype(BF)
        for copy in range(8):
            out_ref[copy, h * 16 : (h + 1) * 16, :] = joined


def swap(a, axis):
    return lax.ppermute(a, axis, [(0, 1), (1, 0)])


def along(a, step):
    return lax.ppermute(a, Z, [(i, (i + step) % 8) for i in range(8)])


def exchange(a, axes):
    return lax.all_to_all(a, axes, 0, 0, tiled=True)


def gather(mine):
    two = ((2, 3, ROWS, HALF), BF, pltpu.VMEM)
    six = ((6, 3, ROWS, HALF), BF, pltpu.VMEM)
    same = exchange(mine, ZQ)
    left, right, early, late = call(cut_kernel, [two] * 4, [VMEM], same)
    same_other = swap(same, CORE)
    left, right, early = along(left, 1), along(right, -1), swap(early, LO)
    left, right, early, late = lax.optimization_barrier((left, right, early, late))
    early_left, early_right, late = along(early, 1), along(early, -1), swap(late, LO)
    middle = call(pack_kernel, six, [VMEM] * 3, left, right, early)
    middle_other = swap(middle, CORE)
    last = call(pack_kernel, six, [VMEM] * 3, early_left, early_right, late)
    return same, middle, last, same_other, middle_other, swap(last, CORE)


def shards(layer_deltas, tap_layers, norm_gain, fc_weight):
    pieces = ((8, 3, ROWS, HALF), BF, pltpu.VMEM)
    sources = [pltpu.with_memory_space_constraint(a, pltpu.HBM) for a in (tap_layers, layer_deltas, norm_gain)]
    sent, taps, deltas, gain = call(
        send_kernel,
        [
            pieces,
            (tap_layers.shape, jnp.int32, pltpu.SMEM),
            (layer_deltas.shape, BF, pltpu.VMEM),
            (norm_gain.shape, F32, pltpu.VMEM),
        ],
        [HBM] * 3,
        *sources,
        scratch=[pltpu.SemaphoreType.DMA((3,))],
    )
    other = swap(sent, CORE)
    paired = call(pair_kernel, pieces, [SMEM, VMEM, VMEM], taps, deltas, other)
    parts = exchange(paired, Z)
    mine = call(tapped_kernel, ((4, 3, ROWS, HALF), BF, pltpu.VMEM), [VMEM, VMEM], parts, gain)
    states = gather(mine)
    partial = call(
        join_kernel,
        ((8, 112, 512), BF, pltpu.VMEM),
        [VMEM] * 8,
        *states,
        fc_weight,
        gain,
        flops=2 * 256 * 6144 * 512,
        scratch=[pltpu.VMEM((256, HALF), BF)],
    )
    partial = exchange(partial, (HI, X))
    joined = call(scale_kernel, ((8, 32, 512), BF, pltpu.VMEM), [VMEM], partial)
    return exchange(joined, (HI, X)).reshape(256, 512)


def solution(mesh):
    fine = Mesh(mesh.devices.reshape(4, 2, 2, 2, 4, 2), (ZQ, ZP, CORE, HI, X, LO))
    section, tensor = (ZQ, ZP, CORE), (HI, X)
    in_specs = (P(section, LO, tensor), P(), P(None, tensor), P(None, tensor, (*section, LO)))
    out_specs = P(None, (*section, LO))
    return jax.shard_map(shards, mesh=fine, in_specs=in_specs, out_specs=out_specs, check_vma=False)
```

time: 118 us -> 109 us (0.924)
  blocking collectives: 99.3 us -> 74 us
  starting transfers between devices: 6.42 us -> 22.2 us
  waiting for transfers between devices: 4.95 us -> 7.54 us
  local copies, waits for them, and re-layouts: 2.59 us -> 0.71 us
    all_to_all x4, blocking collectives: 99.3 us -> 74 us  [exchange(): return lax.all_to_all(a, axes, 0, 0, tiled=True)]
    ppermute x2 -> x6, starting transfers between devices: 6.42 us -> 18 us  [swap(): return lax.ppermute(a, axis, [(0, 1), (1, 0)])]
    ppermute x0 -> x4, starting transfers between devices: none -> 4.21 us  [along(): return lax.ppermute(a, Z, [(i, (i + step) % 8) for i in range(8)])]
    unnamed x9 -> x3, local copies, waits for them, and re-layouts: 2.59 us -> 0.71 us
    ppermute x0 -> x4, waiting for transfers between devices: none -> 1.76 us  [along(): return lax.ppermute(a, Z, [(i, (i + step) % 8) for i in range(8)])]
    ppermute x2 -> x6, waiting for transfers between devices: 4.95 us -> 5.77 us  [swap(): return lax.ppermute(a, axis, [(0, 1), (1, 0)])]
    pallas_call x5 -> x8, Pallas kernels: 4.11 us -> 4.64 us  [call(): pl.pallas_call(kernel, out_shape=[space(shape, kind) for shape, kind, spa...]
  transfers between devices with their start and end apart: 2 -> 10, of which waited for: 2 -> 4; matrix products, arithmetic and copies ran while one was open for 0% -> 0% of each run, Pallas kernels for 0% -> 0%
where the time goes in v2:
time: 109 us
  blocking collectives  74 us (68%)
  starting transfers between devices  22.2 us (20%)
  waiting for transfers between devices  7.54 us (7%)
  Pallas kernels  4.64 us (4%)
    all_to_all x4, blocking collectives, exchange(): return lax.all_to_all(a, axes, 0, 0, tiled=True)  74 us
    ppermute x6, starting transfers between devices, swap(): return lax.ppermute(a, axis, [(0, 1), (1, 0)])  18 us
    ppermute x6, waiting for transfers between devices, swap(): return lax.ppermute(a, axis, [(0, 1), (1, 0)])  5.77 us
    pallas_call x8, Pallas kernels, call(): pl.pallas_call(kernel, out_shape=[space(shape, kind) for shape, kind, spa...  4.64 us
    ppermute x4, starting transfers between devices, along(): return lax.ppermute(a, Z, [(i, (i + step) % 8) for i in range(8)])  4.21 us
  transfers between devices with their start and end apart: 10, of which 4 were waited for; matrix products, arithmetic and copies ran while one was open for 0% of the time, Pallas kernels for 0%

profile of v2, /device:TPU:1, one launch (start us, length us, event | category | flops | bytes accessed | tf_op | source)
XLA Modules:
  0.0 109.2 jit_solution(5030353344802057610)
XLA Ops:
  0.0 0.0 copy-start
  0.0 1.6 %shard_map.46 = (bf16[8,3,16,1024]{3,2,1,0:T(8,128)(2,1)S(1)}, s32[3]{0:T(128)S(4)}, bf16[2,128,2048]{2,1,0:T(8,128)(2,1)S(1)}, f32[3,2048]{1,0:T(4,128)S(1)}) custom-call(s32[3]{0:T(128)} %tap_hbm.1, bf16[2,128,2048]{2,1,0:T(8,128)(2,1)} %delta_hbm.1, f32[3,2048]{1,0:T(4,128)} %gain_hbm.1), custom_call_target="tpu_custom_call" | custom-call | bytes 1073164 | tf_op jit(solution)/shard_map/pallas_call | solution.py:26
  1.6 3.3 %collective-permute-start = (bf16[8,3,16,1024]{3,2,1,0:T(8,128)(2,1)S(1)}, bf16[8,3,16,1024]{3,2,1,0:T(8,128)(2,1)S(1)}, u32[]{:S(2)}, u32[]{:S(2)}) collective-permute-start(bf16[8,3,16,1024]{3,2,1,0:T(8,128)(2,1)S(1)} %get-tuple-element.19), channel_id=1, source_target_pairs={{0,16},{16,0},{1,17},{17,1},{2,18},{18,2},{3,19},{19,3},{4,20},{20... | collective-permute-start | bytes 2359304 | tf_op jit(solution)/shard_map/ppermute | solution.py:176
  5.0 1.9 %collective-permute-done.other_ref = bf16[8,3,16,1024]{3,2,1,0:T(8,128)(2,1)S(1)} collective-permute-done((bf16[8,3,16,1024]{3,2,1,0:T(8,128)(2,1)S(1)}, bf16[8,3,16,1024]{3,2,1,0:T(8,128)(2,1)S(1)}, u32[]{:S(2)}, u32[]{:S(2)}) %collective-permute-start) | collective-permute-done | bytes 786464 | tf_op jit(solution)/shard_map/ppermute | solution.py:176
  6.9 0.3 shard_map.47
  7.2 28.6 %all_to_all.20.parts_ref = bf16[8,3,16,1024]{3,2,1,0:T(8,128)(2,1)S(1)} all-to-all(bf16[8,3,16,1024]{3,2,1,0:T(8,128)(2,1)S(1)} %shard_map.47), channel_id=1, replica_groups=mesh['zq'=4,'zp'=2,'core'=2,'hi'=2,'x'=4,'lo'=2] {'zq','zp'}, dimensions={0} | all-to-all | bytes 1572864 | tf_op jit(solution)/shard_map/all_to_all | solution.py:184
  35.8 0.1 shard_map.48
  35.9 13.3 %all_to_all.21.same_ref.refs_0_ = bf16[4,3,16,1024]{3,2,1,0:T(8,128)(2,1)S(1)} all-to-all(bf16[4,3,16,1024]{3,2,1,0:T(8,128)(2,1)S(1)} %shard_map.48), channel_id=1, replica_groups=mesh['zq'=4,'zp'=2,'core'=2,'hi'=2,'x'=4,'lo'=2] {'zq'}, dimensions={0} | all-to-all | bytes 786432 | tf_op jit(solution)/shard_map/all_to_all | solution.py:184
  49.2 0.1 shard_map.49
  49.3 0.1 collective-permute-start.1
  49.3 2.7 %collective-permute-start.2 = (bf16[2,3,16,1024]{3,2,1,0:T(8,128)(2,1)S(1)}, bf16[2,3,16,1024]{3,2,1,0:T(8,128)(2,1)S(1)}, u32[]{:S(2)}, u32[]{:S(2)}) collective-permute-start(bf16[2,3,16,1024]{3,2,1,0:T(8,128)(2,1)S(1)} %get-tuple-element.22), channel_id=1, source_target_pairs={{0,224},{32,0},{64,32},{96,64},{128,96},{160,128},{192,160},{224,1... | collective-permute-start | bytes 589832 | tf_op jit(solution)/shard_map/ppermute | solution.py:180
  52.0 1.3 %collective-permute-start.3 = (bf16[2,3,16,1024]{3,2,1,0:T(8,128)(2,1)S(1)}, bf16[2,3,16,1024]{3,2,1,0:T(8,128)(2,1)S(1)}, u32[]{:S(2)}, u32[]{:S(2)}) collective-permute-start(bf16[2,3,16,1024]{3,2,1,0:T(8,128)(2,1)S(1)} %get-tuple-element.23), channel_id=1, source_target_pairs={{0,1},{1,0},{2,3},{3,2},{4,5},{5,4},{6,7},{7,6},{8,9},{9,8},{10,11... | collective-permute-start | bytes 589832 | tf_op jit(solution)/shard_map/ppermute | solution.py:176
  53.3 1.8 %collective-permute-done.1.refs_0_ = bf16[2,3,16,1024]{3,2,1,0:T(8,128)(2,1)S(1)} collective-permute-done((bf16[2,3,16,1024]{3,2,1,0:T(8,128)(2,1)S(1)}, bf16[2,3,16,1024]{3,2,1,0:T(8,128)(2,1)S(1)}, u32[]{:S(2)}, u32[]{:S(2)}) %collective-permute-start.1) | collective-permute-done | bytes 196640 | tf_op jit(solution)/shard_map/ppermute | solution.py:180
  55.1 0.0 collective-permute-done.2.refs_1_
  55.1 1.8 %collective-permute-done.3.refs_2_ = bf16[2,3,16,1024]{3,2,1,0:T(8,128)(2,1)S(1)} collective-permute-done((bf16[2,3,16,1024]{3,2,1,0:T(8,128)(2,1)S(1)}, bf16[2,3,16,1024]{3,2,1,0:T(8,128)(2,1)S(1)}, u32[]{:S(2)}, u32[]{:S(2)}) %collective-permute-start.3) | collective-permute-done | bytes 196640 | tf_op jit(solution)/shard_map/ppermute | solution.py:176
  56.8 1.3 %collective-permute-start.6 = (bf16[2,3,16,1024]{3,2,1,0:T(8,128)(2,1)S(1)}, bf16[2,3,16,1024]{3,2,1,0:T(8,128)(2,1)S(1)}, u32[]{:S(2)}, u32[]{:S(2)}) collective-permute-start(bf16[2,3,16,1024]{3,2,1,0:T(8,128)(2,1)S(1)} %get-tuple-element.28), channel_id=1, source_target_pairs={{0,1},{1,0},{2,3},{3,2},{4,5},{5,4},{6,7},{7,6},{8,9},{9,8},{10,11... | collective-permute-start | bytes 589832 | tf_op jit(solution)/shard_map/ppermute | solution.py:176
  58.1 0.9 collective-permute-start.5
  59.0 0.5 collective-permute-start.4
  59.6 7.2 %collective-permute-start.8 = (bf16[6,3,16,1024]{3,2,1,0:T(8,128)(2,1)S(1)}, bf16[6,3,16,1024]{3,2,1,0:T(8,128)(2,1)S(1)}, u32[]{:S(2)}, u32[]{:S(2)}) collective-permute-start(bf16[6,3,16,1024]{3,2,1,0:T(8,128)(2,1)S(1)} %shard_map.50.refs_1_), channel_id=1, source_target_pairs={{0,16},{16,0},{1,17},{17,1},{2,18},{18,2},{3,19},{19,3},{4,20},{20... | collective-permute-start | bytes 1769480 | tf_op jit(solution)/shard_map/ppermute | solution.py:176
  66.8 0.0 collective-permute-done.6.refs_2_
  66.8 0.0 collective-permute-done.5.refs_1_
  66.8 0.0 collective-permute-done.4.refs_0_
  66.9 4.8 %collective-permute-start.9 = (bf16[6,3,16,1024]{3,2,1,0:T(8,128)(2,1)S(1)}, bf16[6,3,16,1024]{3,2,1,0:T(8,128)(2,1)S(1)}, u32[]{:S(2)}, u32[]{:S(2)}) collective-permute-start(bf16[6,3,16,1024]{3,2,1,0:T(8,128)(2,1)S(1)} %shard_map.51.refs_2_), channel_id=1, source_target_pairs={{0,16},{16,0},{1,17},{17,1},{2,18},{18,2},{3,19},{19,3},{4,20},{20... | collective-permute-start | bytes 1769480 | tf_op jit(solution)/shard_map/ppermute | solution.py:176
  71.7 0.1 collective-permute-start.7
  71.8 2.1 %collective-permute-done.7.refs_3_ = bf16[4,3,16,1024]{3,2,1,0:T(8,128)(2,1)S(1)} collective-permute-done((bf16[4,3,16,1024]{3,2,1,0:T(8,128)(2,1)S(1)}, bf16[4,3,16,1024]{3,2,1,0:T(8,128)(2,1)S(1)}, u32[]{:S(2)}, u32[]{:S(2)}) %collective-permute-start.7) | collective-permute-done | bytes 393248 | tf_op jit(solution)/shard_map/ppermute | solution.py:176
  73.8 0.0 collective-permute-done.8.refs_4_
  73.9 0.0 collective-permute-done.9.refs_5_
  73.9 0.0 copy-done
  73.9 2.3 %shard_map.52 = bf16[8,112,512]{2,1,0:T(8,128)(2,1)S(1)} custom-call(bf16[4,3,16,1024]{3,2,1,0:T(8,128)(2,1)S(1)} %all_to_all.21.same_ref.refs_0_, bf16[6,3,16,1024]{3,2,1,0:T(8,128)(2,1)S(1)} %shard_map.50.refs_1_, bf16[6,3,16,1024]{3,2,1,0:T(8,128)(2,1)S(1)} %shard_map.51.refs_2_, bf16[4,3,16,1024]{3,2,1,0:T(8,128)(2,1)S(1)} %collective-permute-done.7.refs_3_, ...), custom_call_target="tpu_custom_call" | custom-call | flops 1610612736 | bytes 9461760 | tf_op jit(solution)/shard_map/pallas_call | solution.py:26
  76.2 21.7 %all_to_all.22.parts_ref = bf16[8,112,512]{2,1,0:T(8,128)(2,1)S(1)} all-to-all(bf16[8,112,512]{2,1,0:T(8,128)(2,1)S(1)} %shard_map.52), channel_id=1, replica_groups=mesh['zq'=4,'zp'=2,'core'=2,'hi'=2,'x'=4,'lo'=2] {'hi','x'}, dimensions={0} | all-to-all | bytes 1835008 | tf_op jit(solution)/shard_map/all_to_all | solution.py:184
  97.9 0.1 shard_map.53
  98.0 10.4 %all_to_all.23 = bf16[8,32,512]{2,1,0:T(8,128)(2,1)S(1)} all-to-all(bf16[8,32,512]{2,1,0:T(8,128)(2,1)S(1)} %shard_map.53), channel_id=1, replica_groups=mesh['zq'=4,'zp'=2,'core'=2,'hi'=2,'x'=4,'lo'=2] {'hi','x'}, dimensions={0} | all-to-all | bytes 524288 | tf_op jit(solution)/shard_map/all_to_all | solution.py:184
  108.4 0.7 copy.6
  (2 shorter events, 0.1 us)
Async XLA Ops:
  0.0 73.9 %copy-start = (bf16[3,2048,512]{2,1,0:T(8,128)(2,1)S(1)}, bf16[3,2048,512]{2,1,0:T(8,128)(2,1)}, u32[]{:S(2)}) copy-start(bf16[3,2048,512]{2,1,0:T(8,128)(2,1)} %refs_6_.1) | copy-start | bytes 18874372
  1.6 5.2 %collective-permute-start = (bf16[8,3,16,1024]{3,2,1,0:T(8,128)(2,1)S(1)}, bf16[8,3,16,1024]{3,2,1,0:T(8,128)(2,1)S(1)}, u32[]{:S(2)}, u32[]{:S(2)}) collective-permute-start(bf16[8,3,16,1024]{3,2,1,0:T(8,128)(2,1)S(1)} %get-tuple-element.19), channel_id=1, source_target_pairs={{0,16},{16,0},{1,17},{17,1},{2,18},{18,2},{3,19},{19,3},{4,20},{20... | collective-permute-start | bytes 2359304 | tf_op jit(solution)/shard_map/ppermute | solution.py:176
  49.3 5.8 %collective-permute-start.1 = (bf16[2,3,16,1024]{3,2,1,0:T(8,128)(2,1)S(1)}, bf16[2,3,16,1024]{3,2,1,0:T(8,128)(2,1)S(1)}, u32[]{:S(2)}, u32[]{:S(2)}) collective-permute-start(bf16[2,3,16,1024]{3,2,1,0:T(8,128)(2,1)S(1)} %get-tuple-element.21), channel_id=1, source_target_pairs={{0,32},{32,64},{64,96},{96,128},{128,160},{160,192},{192,224},{224... | collective-permute-start | bytes 589832 | tf_op jit(solution)/shard_map/ppermute | solution.py:180
  49.3 5.7 %collective-permute-start.2 = (bf16[2,3,16,1024]{3,2,1,0:T(8,128)(2,1)S(1)}, bf16[2,3,16,1024]{3,2,1,0:T(8,128)(2,1)S(1)}, u32[]{:S(2)}, u32[]{:S(2)}) collective-permute-start(bf16[2,3,16,1024]{3,2,1,0:T(8,128)(2,1)S(1)} %get-tuple-element.22), channel_id=1, source_target_pairs={{0,224},{32,0},{64,32},{96,64},{128,96},{160,128},{192,160},{224,1... | collective-permute-start | bytes 589832 | tf_op jit(solution)/shard_map/ppermute | solution.py:180
  52.0 4.8 %collective-permute-start.3 = (bf16[2,3,16,1024]{3,2,1,0:T(8,128)(2,1)S(1)}, bf16[2,3,16,1024]{3,2,1,0:T(8,128)(2,1)S(1)}, u32[]{:S(2)}, u32[]{:S(2)}) collective-permute-start(bf16[2,3,16,1024]{3,2,1,0:T(8,128)(2,1)S(1)} %get-tuple-element.23), channel_id=1, source_target_pairs={{0,1},{1,0},{2,3},{3,2},{4,5},{5,4},{6,7},{7,6},{8,9},{9,8},{10,11... | collective-permute-start | bytes 589832 | tf_op jit(solution)/shard_map/ppermute | solution.py:176
  56.8 10.0 %collective-permute-start.6 = (bf16[2,3,16,1024]{3,2,1,0:T(8,128)(2,1)S(1)}, bf16[2,3,16,1024]{3,2,1,0:T(8,128)(2,1)S(1)}, u32[]{:S(2)}, u32[]{:S(2)}) collective-permute-start(bf16[2,3,16,1024]{3,2,1,0:T(8,128)(2,1)S(1)} %get-tuple-element.28), channel_id=1, source_target_pairs={{0,1},{1,0},{2,3},{3,2},{4,5},{5,4},{6,7},{7,6},{8,9},{9,8},{10,11... | collective-permute-start | bytes 589832 | tf_op jit(solution)/shard_map/ppermute | solution.py:176
  58.1 8.7 %collective-permute-start.5 = (bf16[2,3,16,1024]{3,2,1,0:T(8,128)(2,1)S(1)}, bf16[2,3,16,1024]{3,2,1,0:T(8,128)(2,1)S(1)}, u32[]{:S(2)}, u32[]{:S(2)}) collective-permute-start(bf16[2,3,16,1024]{3,2,1,0:T(8,128)(2,1)S(1)} %collective-permute-done.3.refs_2_), channel_id=1, source_target_pairs={{0,224},{32,0},{64,32},{96,64},{128,96},{160,128},{192,160},{224,1... | collective-permute-start | bytes 589832 | tf_op jit(solution)/shard_map/ppermute | solution.py:180
  59.0 7.8 %collective-permute-start.4 = (bf16[2,3,16,1024]{3,2,1,0:T(8,128)(2,1)S(1)}, bf16[2,3,16,1024]{3,2,1,0:T(8,128)(2,1)S(1)}, u32[]{:S(2)}, u32[]{:S(2)}) collective-permute-start(bf16[2,3,16,1024]{3,2,1,0:T(8,128)(2,1)S(1)} %collective-permute-done.3.refs_2_), channel_id=1, source_target_pairs={{0,32},{32,64},{64,96},{96,128},{128,160},{160,192},{192,224},{224... | collective-permute-start | bytes 589832 | tf_op jit(solution)/shard_map/ppermute | solution.py:180
  59.6 14.2 %collective-permute-start.8 = (bf16[6,3,16,1024]{3,2,1,0:T(8,128)(2,1)S(1)}, bf16[6,3,16,1024]{3,2,1,0:T(8,128)(2,1)S(1)}, u32[]{:S(2)}, u32[]{:S(2)}) collective-permute-start(bf16[6,3,16,1024]{3,2,1,0:T(8,128)(2,1)S(1)} %shard_map.50.refs_1_), channel_id=1, source_target_pairs={{0,16},{16,0},{1,17},{17,1},{2,18},{18,2},{3,19},{19,3},{4,20},{20... | collective-permute-start | bytes 1769480 | tf_op jit(solution)/shard_map/ppermute | solution.py:176
  66.9 7.0 %collective-permute-start.9 = (bf16[6,3,16,1024]{3,2,1,0:T(8,128)(2,1)S(1)}, bf16[6,3,16,1024]{3,2,1,0:T(8,128)(2,1)S(1)}, u32[]{:S(2)}, u32[]{:S(2)}) collective-permute-start(bf16[6,3,16,1024]{3,2,1,0:T(8,128)(2,1)S(1)} %shard_map.51.refs_2_), channel_id=1, source_target_pairs={{0,16},{16,0},{1,17},{17,1},{2,18},{18,2},{3,19},{19,3},{4,20},{20... | collective-permute-start | bytes 1769480 | tf_op jit(solution)/shard_map/ppermute | solution.py:176
  71.7 2.2 %collective-permute-start.7 = (bf16[4,3,16,1024]{3,2,1,0:T(8,128)(2,1)S(1)}, bf16[4,3,16,1024]{3,2,1,0:T(8,128)(2,1)S(1)}, u32[]{:S(2)}, u32[]{:S(2)}) collective-permute-start(bf16[4,3,16,1024]{3,2,1,0:T(8,128)(2,1)S(1)} %all_to_all.21.same_ref.refs_0_), channel_id=1, source_target_pairs={{0,16},{16,0},{1,17},{17,1},{2,18},{18,2},{3,19},{19,3},{4,20},{20... | collective-permute-start | bytes 1179656 | tf_op jit(solution)/shard_map/ppermute | solution.py:176

commit v3 on v2

--- a/solution.py
+++ b/solution.py
@@ -17,6 +17,7 @@
 VMEM = pl.BlockSpec(memory_space=pltpu.VMEM)
 SMEM = pl.BlockSpec(memory_space=pltpu.SMEM)
 HBM = pl.BlockSpec(memory_space=pltpu.HBM)
+ANY = pl.BlockSpec(memory_space=pl.ANY)
 
 
 def call(kernel, shapes, specs, *args, flops=0, limit=24, scratch=()):
@@ -39,51 +40,61 @@
     return pl.ds(pl.multiple_of(core * HALF, HALF), HALF)
 
 
-def segments(tap_ref, delta_ref, tokens, columns):
-    section = lax.axis_index(ZQ) * 4 + lax.axis_index(ZP) * 2 + lax.axis_index(CORE)
-    first = section * 2
-    layers = [delta_ref[j, tokens, columns].astype(F32) for j in range(2)]
-    out = []
-    for k in range(3):
-        total = None
-        for j in range(2):
-            inside = first + j <= tap_ref[k]
-            if k:
-                inside = jnp.logical_and(inside, first + j > tap_ref[k - 1])
-            term = layers[j] * jnp.where(inside, 1.0, 0.0).astype(F32)
-            total = term if total is None else total + term
-        out.append(total)
-    return out
-
-
-def send_kernel(tap_hbm, delta_hbm, gain_hbm, out_ref, tap_ref, delta_ref, gain_ref, sems):
-    columns = half_of(1 - lax.axis_index(CORE))
-    pairs = ((tap_hbm, tap_ref), (delta_hbm, delta_ref), (gain_hbm, gain_ref))
+def segment(layer, tap_ref):
+    return (layer > tap_ref[0]).astype(jnp.int32) + (layer > tap_ref[1]).astype(jnp.int32)
+
+
+def load_kernel(tap_hbm, delta_hbm, gain_hbm, other_ref, mine_ref, tap_ref, gain_ref, three_ref, sems):
+    core = lax.axis_index(CORE)
+    pairs = (
+        (delta_hbm.at[:, :, half_of(1 - core)], other_ref),
+        (delta_hbm.at[:, :, half_of(core)], mine_ref),
+        (tap_hbm, tap_ref),
+        (gain_hbm, gain_ref),
+    )
     copies = [pltpu.make_async_copy(a, b, sems.at[i]) for i, (a, b) in enumerate(pairs)]
     for copy in copies:
         copy.start()
     for copy in copies:
         copy.wait()
+    three_ref[0] = (tap_ref[0] // 4 == tap_ref[1] // 4).astype(jnp.int32)
+
+
+def pair_kernel(tap_ref, mine_ref, other_ref, ends_ref, middle_ref):
+    core = lax.axis_index(CORE)
+    first = (lax.axis_index(ZQ) * 2 + lax.axis_index(ZP)) * 4
+    head, tail = segment(first, tap_ref), segment(first + 3, tap_ref)
+    weights = []
+    for side in (core, 1 - core):
+        for j in range(2):
+            at = segment(first + 2 * side + j, tap_ref)
+            in_head = at == head
+            in_tail = jnp.logical_and(at == tail, tail != head)
+            between = jnp.logical_not(jnp.logical_or(in_head, in_tail))
+            weights.append([jnp.where(w, 1.0, 0.0).astype(F32) for w in (in_head, in_tail, between)])
     for piece in range(8):
-        for k, part in enumerate(segments(tap_ref, delta_ref, pl.ds(piece * ROWS, ROWS), columns)):
-            out_ref[piece, k] = part.astype(BF)
-
-
-def pair_kernel(tap_ref, delta_ref, other_ref, out_ref):
+        rows = slice(piece * ROWS, (piece + 1) * ROWS)
+        layers = [ref[j, rows].astype(F32) for ref in (mine_ref, other_ref) for j in range(2)]
+        sums = []
+        for part in range(3):
+            terms = [layer * weight[part] for layer, weight in zip(layers, weights)]
+            sums.append(((terms[0] + terms[1]) + (terms[2] + terms[3])).astype(BF))
+        ends_ref[piece, 0] = sums[0]
+        ends_ref[piece, 1] = sums[1]
+        middle_ref[piece] = sums[2]
+
+
+def tapped_kernel(tap_ref, ends_ref, middle_ref, gain_ref, out_ref):
     columns = half_of(lax.axis_index(CORE))
-    for piece in range(8):
-        for k, part in enumerate(segments(tap_ref, delta_ref, pl.ds(piece * ROWS, ROWS), columns)):
-            out_ref[piece, k] = (part + other_ref[piece, k].astype(F32)).astype(BF)
-
-
-def tapped_kernel(parts_ref, gain_ref, out_ref):
-    columns = half_of(lax.axis_index(CORE))
-    state = None
+    between = middle_ref[0].astype(F32)
+    for chip in range(1, 8):
+        between = between + middle_ref[chip].astype(F32)
     for k in range(3):
-        total = parts_ref[0, k].astype(F32)
-        for piece in range(1, 8):
-            total = total + parts_ref[piece, k].astype(F32)
-        state = total if state is None else state + total
+        state = between if k else jnp.zeros_like(between)
+        for chip in range(8):
+            for end in range(2):
+                inside = jnp.where(4 * chip + 3 * end <= tap_ref[k], 1.0, 0.0).astype(F32)
+                state = state + ends_ref[chip, end].astype(F32) * inside
         scaled = (state * gain_ref[pl.ds(k, 1), columns]).astype(BF)
         for copy in range(out_ref.shape[0]):
             out_ref[copy, k] = scaled
@@ -112,8 +123,15 @@
 
 
 def pack_kernel(*refs):
-    for i, ref in enumerate(refs[:-1]):
+    for i, ref in enumerate(refs[:3]):
         refs[-1][2 * i : 2 * i + 2] = ref[...]
+
+
+def fetch_kernel(weight_hbm, after_ref, weight_ref, sem):
+    del after_ref
+    copy = pltpu.make_async_copy(weight_hbm, weight_ref, sem)
+    copy.start()
+    copy.wait()
 
 
 def join_kernel(*refs):
@@ -184,7 +202,7 @@
     return lax.all_to_all(a, axes, 0, 0, tiled=True)
 
 
-def gather(mine):
+def gather(mine, weight):
     two = ((2, 3, ROWS, HALF), BF, pltpu.VMEM)
     six = ((6, 3, ROWS, HALF), BF, pltpu.VMEM)
     same = exchange(mine, ZQ)
@@ -195,36 +213,59 @@
     early_left, early_right, late = along(early, 1), along(early, -1), swap(late, LO)
     middle = call(pack_kernel, six, [VMEM] * 3, left, right, early)
     middle_other = swap(middle, CORE)
-    last = call(pack_kernel, six, [VMEM] * 3, early_left, early_right, late)
-    return same, middle, last, same_other, middle_other, swap(last, CORE)
+    weight = call(
+        fetch_kernel,
+        (weight.shape, BF, pltpu.VMEM),
+        [HBM, ANY],
+        pltpu.with_memory_space_constraint(weight, pltpu.HBM),
+        middle,
+        scratch=[pltpu.SemaphoreType.DMA],
+    )
+    last = call(pack_kernel, six, [VMEM] * 3 + [ANY], early_left, early_right, late, weight)
+    return same, middle, last, same_other, middle_other, swap(last, CORE), weight
 
 
 def shards(layer_deltas, tap_layers, norm_gain, fc_weight):
-    pieces = ((8, 3, ROWS, HALF), BF, pltpu.VMEM)
+    raw = ((2, 128, HALF), BF, pltpu.VMEM)
     sources = [pltpu.with_memory_space_constraint(a, pltpu.HBM) for a in (tap_layers, layer_deltas, norm_gain)]
-    sent, taps, deltas, gain = call(
-        send_kernel,
+    sent, own, taps, gain, three = call(
+        load_kernel,
         [
-            pieces,
+            raw,
+            raw,
             (tap_layers.shape, jnp.int32, pltpu.SMEM),
-            (layer_deltas.shape, BF, pltpu.VMEM),
             (norm_gain.shape, F32, pltpu.VMEM),
+            ((1,), jnp.int32, pltpu.SMEM),
         ],
         [HBM] * 3,
         *sources,
-        scratch=[pltpu.SemaphoreType.DMA((3,))],
-    )
-    other = swap(sent, CORE)
-    paired = call(pair_kernel, pieces, [SMEM, VMEM, VMEM], taps, deltas, other)
-    parts = exchange(paired, Z)
-    mine = call(tapped_kernel, ((4, 3, ROWS, HALF), BF, pltpu.VMEM), [VMEM, VMEM], parts, gain)
-    states = gather(mine)
+        scratch=[pltpu.SemaphoreType.DMA((4,))],
+    )
+    ends, middle = call(
+        pair_kernel,
+        [((8, 2, ROWS, HALF), BF, pltpu.VMEM), ((8, ROWS, HALF), BF, pltpu.VMEM)],
+        [SMEM, VMEM, VMEM],
+        taps,
+        own,
+        swap(sent, CORE),
+    )
+    ends = exchange(ends, Z)
+    middle = lax.cond(three[0] != 0, lambda a: exchange(a, Z), lambda a: a, middle)
+    mine = call(
+        tapped_kernel,
+        ((4, 3, ROWS, HALF), BF, pltpu.VMEM),
+        [SMEM, VMEM, VMEM, VMEM],
+        taps,
+        ends,
+        middle,
+        gain,
+    )
+    states = gather(mine, fc_weight)
     partial = call(
         join_kernel,
         ((8, 112, 512), BF, pltpu.VMEM),
         [VMEM] * 8,
         *states,
-        fc_weight,
         gain,
         flops=2 * 256 * 6144 * 512,
         scratch=[pltpu.VMEM((256, HALF), BF)],

time: 109 us -> 103 us (0.945)
  blocking collectives: 74 us -> 68.4 us
  Pallas kernels: 4.64 us -> 7.44 us
  starting transfers between devices: 22.2 us -> 19.4 us
    all_to_all x4, blocking collectives: 74 us -> 68.4 us  [exchange(): return lax.all_to_all(a, axes, 0, 0, tiled=True)]
    pallas_call x8 -> x9, Pallas kernels: 4.64 us -> 7.44 us  [call(): pl.pallas_call(kernel, out_shape=[space(shape, kind) for shape, kind, spa...]
    ppermute x6, starting transfers between devices: 18 us -> 15.2 us  [swap(): return lax.ppermute(a, axis, [(0, 1), (1, 0)])]
  transfers between devices with their start and end apart: 10 -> 10, of which waited for: 4 -> 4; matrix products, arithmetic and copies ran while one was open for 0% -> 0% of each run, Pallas kernels for 0% -> 3%
where the time goes in v3:
time: 103 us
  blocking collectives  68.4 us (66%)
  starting transfers between devices  19.4 us (19%)
  Pallas kernels  7.44 us (7%)
  waiting for transfers between devices  7.16 us (7%)
    all_to_all x4, blocking collectives, exchange(): return lax.all_to_all(a, axes, 0, 0, tiled=True)  68.4 us
    ppermute x6, starting transfers between devices, swap(): return lax.ppermute(a, axis, [(0, 1), (1, 0)])  15.2 us
    pallas_call x9, Pallas kernels, call(): pl.pallas_call(kernel, out_shape=[space(shape, kind) for shape, kind, spa...  7.44 us
    ppermute x6, waiting for transfers between devices, swap(): return lax.ppermute(a, axis, [(0, 1), (1, 0)])  5.4 us
    ppermute x4, starting transfers between devices, along(): return lax.ppermute(a, Z, [(i, (i + step) % 8) for i in range(8)])  4.21 us
  transfers between devices with their start and end apart: 10, of which 4 were waited for; matrix products, arithmetic and copies ran while one was open for 0% of the time, Pallas kernels for 3%

profile of v3, /device:TPU:1, one launch (start us, length us, event | category | flops | bytes accessed | tf_op | source)
XLA Modules:
  0.0 103.2 jit_solution(1773105060738474608)
XLA Ops:
  0.0 1.3 %shard_map.46 = (bf16[2,128,1024]{2,1,0:T(8,128)(2,1)S(1)}, bf16[2,128,1024]{2,1,0:T(8,128)(2,1)S(1)}, s32[3]{0:T(128)S(4)}, f32[3,2048]{1,0:T(4,128)S(1)}, s32[1]{0:T(128)S(4)}) custom-call(s32[3]{0:T(128)} %tap_hbm.1, bf16[2,128,2048]{2,1,0:T(8,128)(2,1)} %delta_hbm.1, f32[3,2048]{1,0:T(4,128)} %gain_hbm.1), custom_call_target="tpu_custom_call" | custom-call | bytes 1073164 | tf_op jit(solution)/shard_map/pallas_call | solution.py:27
  1.3 3.3 %collective-permute-start = (bf16[2,128,1024]{2,1,0:T(8,128)(2,1)S(1)}, bf16[2,128,1024]{2,1,0:T(8,128)(2,1)S(1)}, u32[]{:S(2)}, u32[]{:S(2)}) collective-permute-start(bf16[2,128,1024]{2,1,0:T(8,128)(2,1)S(1)} %get-tuple-element.27), channel_id=1, source_target_pairs={{0,16},{16,0},{1,17},{17,1},{2,18},{18,2},{3,19},{19,3},{4,20},{20... | collective-permute-start | bytes 1572872 | tf_op jit(solution)/shard_map/ppermute | solution.py:194
  4.6 1.5 %collective-permute-done.other_ref = bf16[2,128,1024]{2,1,0:T(8,128)(2,1)S(1)} collective-permute-done((bf16[2,128,1024]{2,1,0:T(8,128)(2,1)S(1)}, bf16[2,128,1024]{2,1,0:T(8,128)(2,1)S(1)}, u32[]{:S(2)}, u32[]{:S(2)}) %collective-permute-start) | collective-permute-done | bytes 524320 | tf_op jit(solution)/shard_map/ppermute | solution.py:194
  6.1 0.5 shard_map.47
  6.6 22.9 %all_to_all.25.ends_ref = bf16[8,2,16,1024]{3,2,1,0:T(8,128)(2,1)S(1)} all-to-all(bf16[8,2,16,1024]{3,2,1,0:T(8,128)(2,1)S(1)} %get-tuple-element.28), channel_id=1, replica_groups=mesh['zq'=4,'zp'=2,'core'=2,'hi'=2,'x'=4,'lo'=2] {'zq','zp'}, dimensions={0} | all-to-all | bytes 1048576 | tf_op jit(solution)/shard_map/all_to_all | solution.py:202
  29.6 0.4 shard_map.48
  29.9 13.3 %all_to_all.26.same_ref.refs_0_ = bf16[4,3,16,1024]{3,2,1,0:T(8,128)(2,1)S(1)} all-to-all(bf16[4,3,16,1024]{3,2,1,0:T(8,128)(2,1)S(1)} %shard_map.48), channel_id=1, replica_groups=mesh['zq'=4,'zp'=2,'core'=2,'hi'=2,'x'=4,'lo'=2] {'zq'}, dimensions={0} | all-to-all | bytes 786432 | tf_op jit(solution)/shard_map/all_to_all | solution.py:202
  43.2 0.1 shard_map.49
  43.3 0.1 collective-permute-start.1
  43.4 2.7 %collective-permute-start.2 = (bf16[2,3,16,1024]{3,2,1,0:T(8,128)(2,1)S(1)}, bf16[2,3,16,1024]{3,2,1,0:T(8,128)(2,1)S(1)}, u32[]{:S(2)}, u32[]{:S(2)}) collective-permute-start(bf16[2,3,16,1024]{3,2,1,0:T(8,128)(2,1)S(1)} %get-tuple-element.33), channel_id=1, source_target_pairs={{0,224},{32,0},{64,32},{96,64},{128,96},{160,128},{192,160},{224,1... | collective-permute-start | bytes 589832 | tf_op jit(solution)/shard_map/ppermute | solution.py:198
  46.0 1.3 %collective-permute-start.3 = (bf16[2,3,16,1024]{3,2,1,0:T(8,128)(2,1)S(1)}, bf16[2,3,16,1024]{3,2,1,0:T(8,128)(2,1)S(1)}, u32[]{:S(2)}, u32[]{:S(2)}) collective-permute-start(bf16[2,3,16,1024]{3,2,1,0:T(8,128)(2,1)S(1)} %get-tuple-element.34), channel_id=1, source_target_pairs={{0,1},{1,0},{2,3},{3,2},{4,5},{5,4},{6,7},{7,6},{8,9},{9,8},{10,11... | collective-permute-start | bytes 589832 | tf_op jit(solution)/shard_map/ppermute | solution.py:194
  47.3 1.8 %collective-permute-done.1.refs_0_ = bf16[2,3,16,1024]{3,2,1,0:T(8,128)(2,1)S(1)} collective-permute-done((bf16[2,3,16,1024]{3,2,1,0:T(8,128)(2,1)S(1)}, bf16[2,3,16,1024]{3,2,1,0:T(8,128)(2,1)S(1)}, u32[]{:S(2)}, u32[]{:S(2)}) %collective-permute-start.1) | collective-permute-done | bytes 196640 | tf_op jit(solution)/shard_map/ppermute | solution.py:198
  49.1 0.0 collective-permute-done.2.refs_1_
  49.1 1.8 %collective-permute-done.3.refs_2_ = bf16[2,3,16,1024]{3,2,1,0:T(8,128)(2,1)S(1)} collective-permute-done((bf16[2,3,16,1024]{3,2,1,0:T(8,128)(2,1)S(1)}, bf16[2,3,16,1024]{3,2,1,0:T(8,128)(2,1)S(1)}, u32[]{:S(2)}, u32[]{:S(2)}) %collective-permute-start.3) | collective-permute-done | bytes 196640 | tf_op jit(solution)/shard_map/ppermute | solution.py:194
  50.9 1.3 %collective-permute-start.6 = (bf16[2,3,16,1024]{3,2,1,0:T(8,128)(2,1)S(1)}, bf16[2,3,16,1024]{3,2,1,0:T(8,128)(2,1)S(1)}, u32[]{:S(2)}, u32[]{:S(2)}) collective-permute-start(bf16[2,3,16,1024]{3,2,1,0:T(8,128)(2,1)S(1)} %get-tuple-element.39), channel_id=1, source_target_pairs={{0,1},{1,0},{2,3},{3,2},{4,5},{5,4},{6,7},{7,6},{8,9},{9,8},{10,11... | collective-permute-start | bytes 589832 | tf_op jit(solution)/shard_map/ppermute | solution.py:194
  52.2 0.9 collective-permute-start.5
  53.1 0.5 collective-permute-start.4
  53.7 7.2 %collective-permute-start.8 = (bf16[6,3,16,1024]{3,2,1,0:T(8,128)(2,1)S(1)}, bf16[6,3,16,1024]{3,2,1,0:T(8,128)(2,1)S(1)}, u32[]{:S(2)}, u32[]{:S(2)}) collective-permute-start(bf16[6,3,16,1024]{3,2,1,0:T(8,128)(2,1)S(1)} %shard_map.50.after_ref.refs_1_), channel_id=1, source_target_pairs={{0,16},{16,0},{1,17},{17,1},{2,18},{18,2},{3,19},{19,3},{4,20},{20... | collective-permute-start | bytes 1769480 | tf_op jit(solution)/shard_map/ppermute | solution.py:194
  60.9 2.8 %shard_map.51.refs_3_.refs_6_ = bf16[3,2048,512]{2,1,0:T(8,128)(2,1)S(1)} custom-call(bf16[3,2048,512]{2,1,0:T(8,128)(2,1)} %weight_hbm.1, bf16[6,3,16,1024]{3,2,1,0:T(8,128)(2,1)S(1)} %shard_map.50.after_ref.refs_1_), custom_call_target="tpu_custom_call" | custom-call | bytes 6881280 | tf_op jit(solution)/shard_map/pallas_call | solution.py:27
  63.7 0.0 collective-permute-done.6.refs_2_
  63.7 0.0 collective-permute-done.5.refs_1_
  63.7 0.0 collective-permute-done.4.refs_0_
  63.8 2.0 %collective-permute-start.9 = (bf16[6,3,16,1024]{3,2,1,0:T(8,128)(2,1)S(1)}, bf16[6,3,16,1024]{3,2,1,0:T(8,128)(2,1)S(1)}, u32[]{:S(2)}, u32[]{:S(2)}) collective-permute-start(bf16[6,3,16,1024]{3,2,1,0:T(8,128)(2,1)S(1)} %shard_map.52.refs_2_), channel_id=1, source_target_pairs={{0,16},{16,0},{1,17},{17,1},{2,18},{18,2},{3,19},{19,3},{4,20},{20... | collective-permute-start | bytes 1769480 | tf_op jit(solution)/shard_map/ppermute | solution.py:194
  65.7 0.1 collective-permute-start.7
  65.8 2.1 %collective-permute-done.7.refs_3_ = bf16[4,3,16,1024]{3,2,1,0:T(8,128)(2,1)S(1)} collective-permute-done((bf16[4,3,16,1024]{3,2,1,0:T(8,128)(2,1)S(1)}, bf16[4,3,16,1024]{3,2,1,0:T(8,128)(2,1)S(1)}, u32[]{:S(2)}, u32[]{:S(2)}) %collective-permute-start.7) | collective-permute-done | bytes 393248 | tf_op jit(solution)/shard_map/ppermute | solution.py:194
  67.9 0.0 collective-permute-done.8.refs_4_
  67.9 0.0 collective-permute-done.9.refs_5_
  67.9 2.3 %shard_map.53 = bf16[8,112,512]{2,1,0:T(8,128)(2,1)S(1)} custom-call(bf16[4,3,16,1024]{3,2,1,0:T(8,128)(2,1)S(1)} %all_to_all.26.same_ref.refs_0_, bf16[6,3,16,1024]{3,2,1,0:T(8,128)(2,1)S(1)} %shard_map.50.after_ref.refs_1_, bf16[6,3,16,1024]{3,2,1,0:T(8,128)(2,1)S(1)} %shard_map.52.refs_2_, bf16[4,3,16,1024]{3,2,1,0:T(8,128)(2,1)S(1)} %collective-permute-done.7.refs_3_, ...), custom_call_target="tpu_custom_call" | custom-call | flops 1610612736 | bytes 9461760 | tf_op jit(solution)/shard_map/pallas_call | solution.py:27
  70.2 21.7 %all_to_all.27.parts_ref = bf16[8,112,512]{2,1,0:T(8,128)(2,1)S(1)} all-to-all(bf16[8,112,512]{2,1,0:T(8,128)(2,1)S(1)} %shard_map.53), channel_id=1, replica_groups=mesh['zq'=4,'zp'=2,'core'=2,'hi'=2,'x'=4,'lo'=2] {'hi','x'}, dimensions={0} | all-to-all | bytes 1835008 | tf_op jit(solution)/shard_map/all_to_all | solution.py:202
  92.0 0.1 shard_map.54
  92.1 10.4 %all_to_all.28 = bf16[8,32,512]{2,1,0:T(8,128)(2,1)S(1)} all-to-all(bf16[8,32,512]{2,1,0:T(8,128)(2,1)S(1)} %shard_map.54), channel_id=1, replica_groups=mesh['zq'=4,'zp'=2,'core'=2,'hi'=2,'x'=4,'lo'=2] {'hi','x'}, dimensions={0} | all-to-all | bytes 524288 | tf_op jit(solution)/shard_map/all_to_all | solution.py:202
  102.5 0.7 copy.9
  (3 shorter events, 0.1 us)
Async XLA Ops:
  1.3 4.9 %collective-permute-start = (bf16[2,128,1024]{2,1,0:T(8,128)(2,1)S(1)}, bf16[2,128,1024]{2,1,0:T(8,128)(2,1)S(1)}, u32[]{:S(2)}, u32[]{:S(2)}) collective-permute-start(bf16[2,128,1024]{2,1,0:T(8,128)(2,1)S(1)} %get-tuple-element.27), channel_id=1, source_target_pairs={{0,16},{16,0},{1,17},{17,1},{2,18},{18,2},{3,19},{19,3},{4,20},{20... | collective-permute-start | bytes 1572872 | tf_op jit(solution)/shard_map/ppermute | solution.py:194
  43.3 5.8 %collective-permute-start.1 = (bf16[2,3,16,1024]{3,2,1,0:T(8,128)(2,1)S(1)}, bf16[2,3,16,1024]{3,2,1,0:T(8,128)(2,1)S(1)}, u32[]{:S(2)}, u32[]{:S(2)}) collective-permute-start(bf16[2,3,16,1024]{3,2,1,0:T(8,128)(2,1)S(1)} %get-tuple-element.32), channel_id=1, source_target_pairs={{0,32},{32,64},{64,96},{96,128},{128,160},{160,192},{192,224},{224... | collective-permute-start | bytes 589832 | tf_op jit(solution)/shard_map/ppermute | solution.py:198
  43.4 5.7 %collective-permute-start.2 = (bf16[2,3,16,1024]{3,2,1,0:T(8,128)(2,1)S(1)}, bf16[2,3,16,1024]{3,2,1,0:T(8,128)(2,1)S(1)}, u32[]{:S(2)}, u32[]{:S(2)}) collective-permute-start(bf16[2,3,16,1024]{3,2,1,0:T(8,128)(2,1)S(1)} %get-tuple-element.33), channel_id=1, source_target_pairs={{0,224},{32,0},{64,32},{96,64},{128,96},{160,128},{192,160},{224,1... | collective-permute-start | bytes 589832 | tf_op jit(solution)/shard_map/ppermute | solution.py:198
  46.0 4.8 %collective-permute-start.3 = (bf16[2,3,16,1024]{3,2,1,0:T(8,128)(2,1)S(1)}, bf16[2,3,16,1024]{3,2,1,0:T(8,128)(2,1)S(1)}, u32[]{:S(2)}, u32[]{:S(2)}) collective-permute-start(bf16[2,3,16,1024]{3,2,1,0:T(8,128)(2,1)S(1)} %get-tuple-element.34), channel_id=1, source_target_pairs={{0,1},{1,0},{2,3},{3,2},{4,5},{5,4},{6,7},{7,6},{8,9},{9,8},{10,11... | collective-permute-start | bytes 589832 | tf_op jit(solution)/shard_map/ppermute | solution.py:194
  50.9 12.8 %collective-permute-start.6 = (bf16[2,3,16,1024]{3,2,1,0:T(8,128)(2,1)S(1)}, bf16[2,3,16,1024]{3,2,1,0:T(8,128)(2,1)S(1)}, u32[]{:S(2)}, u32[]{:S(2)}) collective-permute-start(bf16[2,3,16,1024]{3,2,1,0:T(8,128)(2,1)S(1)} %get-tuple-element.39), channel_id=1, source_target_pairs={{0,1},{1,0},{2,3},{3,2},{4,5},{5,4},{6,7},{7,6},{8,9},{9,8},{10,11... | collective-permute-start | bytes 589832 | tf_op jit(solution)/shard_map/ppermute | solution.py:194
  52.2 11.5 %collective-permute-start.5 = (bf16[2,3,16,1024]{3,2,1,0:T(8,128)(2,1)S(1)}, bf16[2,3,16,1024]{3,2,1,0:T(8,128)(2,1)S(1)}, u32[]{:S(2)}, u32[]{:S(2)}) collective-permute-start(bf16[2,3,16,1024]{3,2,1,0:T(8,128)(2,1)S(1)} %collective-permute-done.3.refs_2_), channel_id=1, source_target_pairs={{0,224},{32,0},{64,32},{96,64},{128,96},{160,128},{192,160},{224,1... | collective-permute-start | bytes 589832 | tf_op jit(solution)/shard_map/ppermute | solution.py:198
  53.1 10.6 %collective-permute-start.4 = (bf16[2,3,16,1024]{3,2,1,0:T(8,128)(2,1)S(1)}, bf16[2,3,16,1024]{3,2,1,0:T(8,128)(2,1)S(1)}, u32[]{:S(2)}, u32[]{:S(2)}) collective-permute-start(bf16[2,3,16,1024]{3,2,1,0:T(8,128)(2,1)S(1)} %collective-permute-done.3.refs_2_), channel_id=1, source_target_pairs={{0,32},{32,64},{64,96},{96,128},{128,160},{160,192},{192,224},{224... | collective-permute-start | bytes 589832 | tf_op jit(solution)/shard_map/ppermute | solution.py:198
  53.7 14.3 %collective-permute-start.8 = (bf16[6,3,16,1024]{3,2,1,0:T(8,128)(2,1)S(1)}, bf16[6,3,16,1024]{3,2,1,0:T(8,128)(2,1)S(1)}, u32[]{:S(2)}, u32[]{:S(2)}) collective-permute-start(bf16[6,3,16,1024]{3,2,1,0:T(8,128)(2,1)S(1)} %shard_map.50.after_ref.refs_1_), channel_id=1, source_target_pairs={{0,16},{16,0},{1,17},{17,1},{2,18},{18,2},{3,19},{19,3},{4,20},{20... | collective-permute-start | bytes 1769480 | tf_op jit(solution)/shard_map/ppermute | solution.py:194
  63.8 4.2 %collective-permute-start.9 = (bf16[6,3,16,1024]{3,2,1,0:T(8,128)(2,1)S(1)}, bf16[6,3,16,1024]{3,2,1,0:T(8,128)(2,1)S(1)}, u32[]{:S(2)}, u32[]{:S(2)}) collective-permute-start(bf16[6,3,16,1024]{3,2,1,0:T(8,128)(2,1)S(1)} %shard_map.52.refs_2_), channel_id=1, source_target_pairs={{0,16},{16,0},{1,17},{17,1},{2,18},{18,2},{3,19},{19,3},{4,20},{20... | collective-permute-start | bytes 1769480 | tf_op jit(solution)/shard_map/ppermute | solution.py:194
  65.7 2.2 %collective-permute-start.7 = (bf16[4,3,16,1024]{3,2,1,0:T(8,128)(2,1)S(1)}, bf16[4,3,16,1024]{3,2,1,0:T(8,128)(2,1)S(1)}, u32[]{:S(2)}, u32[]{:S(2)}) collective-permute-start(bf16[4,3,16,1024]{3,2,1,0:T(8,128)(2,1)S(1)} %all_to_all.26.same_ref.refs_0_), channel_id=1, source_target_pairs={{0,16},{16,0},{1,17},{17,1},{2,18},{18,2},{3,19},{19,3},{4,20},{20... | collective-permute-start | bytes 1179656 | tf_op jit(solution)/shard_map/ppermute | solution.py:194

commit v4 on v3

v4 whole, which is shorter than its diff:
```python
import functools

import jax
import jax.numpy as jnp
from jax import lax
from jax.experimental import pallas as pl
from jax.experimental.pallas import tpu as pltpu
from jax.sharding import Mesh, PartitionSpec as P

D = 16384
EPS = 1e-05
ZQ, ZP, CORE, HI, X, LO = "zq", "zp", "core", "hi", "x", "lo"
Z = (ZQ, ZP)
BF, F32 = jnp.bfloat16, jnp.float32
ROWS = 16
HALF = 1024
MIB = 1 << 20

VMEM = pl.BlockSpec(memory_space=pltpu.VMEM)
SMEM = pl.BlockSpec(memory_space=pltpu.SMEM)
HBM = pl.BlockSpec(memory_space=pltpu.HBM)
ANY = pl.BlockSpec(memory_space=pl.ANY)


def call(kernel, shapes, specs, *args, flops=0, limit=24, scratch=(), alias=None):
    size = sum(a.size * a.dtype.itemsize for a in args)
    single = not isinstance(shapes, list)
    shapes = [shapes] if single else shapes
    out = pl.pallas_call(
        kernel,
        out_shape=[space(shape, kind) for shape, kind, space in shapes],
        in_specs=specs,
        out_specs=[pl.BlockSpec(memory_space=space) for _, _, space in shapes],
        scratch_shapes=list(scratch),
        input_output_aliases=alias or {},
        cost_estimate=pl.CostEstimate(flops=flops, bytes_accessed=size, transcendentals=0),
        compiler_params=pltpu.CompilerParams(vmem_limit_bytes=limit * MIB),
    )(*args)
    return out[0] if single else out


def half_of(core):
    return pl.ds(pl.multiple_of(core * HALF, HALF), HALF)


def segment(layer, tap_ref):
    return (layer > tap_ref[0]).astype(jnp.int32) + (layer > tap_ref[1]).astype(jnp.int32)


def load_kernel(tap_hbm, delta_hbm, gain_hbm, other_ref, mine_ref, tap_ref, gain_ref, three_ref, sems):
    core = lax.axis_index(CORE)
    pairs = (
        (delta_hbm.at[:, :, half_of(1 - core)], other_ref),
        (delta_hbm.at[:, :, half_of(core)], mine_ref),
        (tap_hbm, tap_ref),
        (gain_hbm, gain_ref),
    )
    copies = [pltpu.make_async_copy(a, b, sems.at[i]) for i, (a, b) in enumerate(pairs)]
    for copy in copies:
        copy.start()
    for copy in copies:
        copy.wait()
    three_ref[0] = (tap_ref[0] // 4 == tap_ref[1] // 4).astype(jnp.int32)


def pair_kernel(tap_ref, mine_ref, other_ref, ends_ref, middle_ref):
    core = lax.axis_index(CORE)
    first = (lax.axis_index(ZQ) * 2 + lax.axis_index(ZP)) * 4
    head, tail = segment(first, tap_ref), segment(first + 3, tap_ref)
    weights = []
    for side in (core, 1 - core):
        for j in range(2):
            at = segment(first + 2 * side + j, tap_ref)
            in_head = at == head
            in_tail = jnp.logical_and(at == tail, tail != head)
            between = jnp.logical_not(jnp.logical_or(in_head, in_tail))
            weights.append([jnp.where(w, 1.0, 0.0).astype(F32) for w in (in_head, in_tail, between)])
    for piece in range(8):
        rows = slice(piece * ROWS, (piece + 1) * ROWS)
        layers = [ref[j, rows].astype(F32) for ref in (mine_ref, other_ref) for j in range(2)]
        sums = []
        for part in range(3):
            terms = [layer * weight[part] for layer, weight in zip(layers, weights)]
            sums.append(((terms[0] + terms[1]) + (terms[2] + terms[3])).astype(BF))
        ends_ref[piece, 0] = sums[0]
        ends_ref[piece, 1] = sums[1]
        middle_ref[piece] = sums[2]


def tapped_kernel(tap_ref, ends_ref, middle_ref, gain_ref, out_ref):
    columns = half_of(lax.axis_index(CORE))
    between = middle_ref[0].astype(F32)
    for chip in range(1, 8):
        between = between + middle_ref[chip].astype(F32)
    for k in range(3):
        state = between if k else jnp.zeros_like(between)
        for chip in range(8):
            for end in range(2):
                inside = jnp.where(4 * chip + 3 * end <= tap_ref[k], 1.0, 0.0).astype(F32)
                state = state + ends_ref[chip, end].astype(F32) * inside
        out_ref[0, k] = (state * gain_ref[pl.ds(k, 1), columns]).astype(BF)


def blocks_of():
    z = 2 * lax.axis_index(ZQ) + lax.axis_index(ZP)
    mine = lax.axis_index(LO) * 8
    yours = 8 - mine
    early = [mine + lax.rem(z + step, 8) for step in (0, 6, 2, 4)] + [yours + z]
    early += [mine + lax.rem(z + 7, 8), mine + lax.rem(z + 5, 8), yours + lax.rem(z + 7, 8)]
    early += [mine + lax.rem(z + 1, 8), mine + lax.rem(z + 3, 8), yours + lax.rem(z + 1, 8)]
    early += [yours + lax.rem(z + step, 8) for step in (2, 6, 4)]
    return early, [yours + lax.rem(z + 5, 8), yours + lax.rem(z + 3, 8)]


def cut_kernel(piece, below, above, far, near, right_ref, left_ref, across_ref, head_ref, tail_ref):
    for out_ref, refs in (
        (right_ref, (piece, below, near)),
        (left_ref, (piece, above, near)),
        (across_ref, (above, below, far)),
        (head_ref, (piece, below)),
        (tail_ref, (above, far)),
    ):
        for i, ref in enumerate(refs):
            out_ref[i] = ref[0]


def pack_kernel(count, *refs):
    out_ref = refs[-1]
    at = 0
    for ref in refs[:count]:
        out_ref[at : at + ref.shape[0]] = ref[...]
        at += ref.shape[0]


def ends_kernel(across_ref, left_ref, right_ref):
    left_ref[0] = across_ref[0]
    right_ref[0] = across_ref[1]


def fetch_kernel(weight_hbm, after_ref, weight_ref, sem):
    del after_ref
    copy = pltpu.make_async_copy(weight_hbm, weight_ref, sem)
    copy.start()
    copy.wait()


def join(blocks, sides, weight_ref, gain_ref, out_ref, state_ref):
    lane = lax.broadcasted_iota(jnp.int32, (ROWS, 128), 1) // ROWS
    squares = [[None] * 3 for _ in blocks]
    for k in range(3):
        total = None
        sums = None
        for refs, side in sides:
            at = 0
            for ref in refs:
                rows = ref.shape[0] * ROWS
                state_ref[at : at + rows, :] = ref[:, k].reshape(rows, HALF)
                at += rows
            states = state_ref[...]
            product = jnp.dot(states, weight_ref[k, half_of(side), :], preferred_element_type=F32)
            plain = states.astype(F32) * (1.0 / gain_ref[pl.ds(k, 1), half_of(side)])
            square = jnp.sum(plain * plain, axis=1, keepdims=True)
            total = product if total is None else total + product
            sums = square if sums is None else sums + square
        total = total.astype(BF)
        for i, block in enumerate(blocks):
            rows = slice(i * ROWS, (i + 1) * ROWS)
            squares[i][k] = sums[rows]
            for column in range(4):
                at = pl.multiple_of((k * 4 + column) * 32 + lax.rem(block, 2) * ROWS, ROWS)
                out_ref[block // 2, pl.ds(at, ROWS), :] = total[rows, column * 128 : (column + 1) * 128]
    for i, block in enumerate(blocks):
        packed = out_ref[block // 2, 384:400, :].astype(F32)
        for k in range(3):
            packed = jnp.where(lane == 2 * k + lax.rem(block, 2), squares[i][k], packed)
        out_ref[block // 2, 384:400, :] = packed.astype(BF)


def early_kernel(head, middle, head_other, middle_other, weight_ref, gain_ref, out_ref, state_ref):
    core = lax.axis_index(CORE)
    out_ref[:, 384:400, :] = jnp.zeros((8, ROWS, 128), BF)
    sides = (((head, middle), core), ((head_other, middle_other), 1 - core))
    join(blocks_of()[0], sides, weight_ref, gain_ref, out_ref, state_ref)


def last_kernel(early_ref, last, last_other, weight_ref, gain_ref, out_ref, state_ref):
    del early_ref
    core = lax.axis_index(CORE)
    join(blocks_of()[1], (((last,), core), ((last_other,), 1 - core)), weight_ref, gain_ref, out_ref, state_ref)


def scale_kernel(parts_ref, out_ref):
    squares = parts_ref[0, 384:400, :].astype(F32)
    for piece in range(1, 8):
        squares = squares + parts_ref[piece, 384:400, :].astype(F32)
    scale = lax.rsqrt(squares / D + EPS)
    for h in range(2):
        for column in range(4):
            joined = None
            for k in range(3):
                rows = pl.ds((k * 4 + column) * 32 + h * ROWS, ROWS)
                total = parts_ref[0, rows, :].astype(F32)
                for piece in range(1, 8):
                    total = total + parts_ref[piece, rows, :].astype(F32)
                at = ROWS * (2 * k + h)
                total = total * scale[:, at : at + 1]
                joined = total if joined is None else joined + total
            joined = joined.astype(BF)
            for copy in range(8):
                out_ref[copy, h * ROWS : (h + 1) * ROWS, column * 128 : (column + 1) * 128] = joined


def swap(a, axis):
    return lax.ppermute(a, axis, [(0, 1), (1, 0)])


def along(a, step):
    return lax.ppermute(a, Z, [(i, (i + step) % 8) for i in range(8)])


def exchange(a, axes):
    return lax.all_to_all(a, axes, 0, 0, tiled=True)


def states(count):
    return ((count, 3, ROWS, HALF), BF, pltpu.VMEM)


def shards(layer_deltas, tap_layers, norm_gain, fc_weight):
    raw = ((2, 128, HALF), BF, pltpu.VMEM)
    sources = [pltpu.with_memory_space_constraint(a, pltpu.HBM) for a in (tap_layers, layer_deltas, norm_gain)]
    sent, own, taps, gain, three = call(
        load_kernel,
        [
            raw,
            raw,
            (tap_layers.shape, jnp.int32, pltpu.SMEM),
            (norm_gain.shape, F32, pltpu.VMEM),
            ((1,), jnp.int32, pltpu.SMEM),
        ],
        [HBM] * 3,
        *sources,
        scratch=[pltpu.SemaphoreType.DMA((4,))],
    )
    ends, middle = call(
        pair_kernel,
        [((8, 2, ROWS, HALF), BF, pltpu.VMEM), ((8, ROWS, HALF), BF, pltpu.VMEM)],
        [SMEM, VMEM, VMEM],
        taps,
        own,
        swap(sent, CORE),
    )
    ends = exchange(ends, Z)
    middle = lax.cond(three[0] != 0, lambda a: exchange(a, Z), lambda a: a, middle)
    piece = call(tapped_kernel, states(1), [SMEM, VMEM, VMEM, VMEM], taps, ends, middle, gain)
    far = along(piece, 4)
    below, above = along(piece, 2), along(piece, -2)
    near = swap(piece, LO)
    parts = [states(3)] * 3 + [states(2)] * 2
    right, left, across, head, tail = call(cut_kernel, parts, [VMEM] * 5, piece, below, above, far, near)
    weight = call(
        fetch_kernel,
        (fc_weight.shape, BF, pltpu.VMEM),
        [HBM, ANY],
        pltpu.with_memory_space_constraint(fc_weight, pltpu.HBM),
        across,
        scratch=[pltpu.SemaphoreType.DMA],
    )
    first = (along(right, 1), along(left, -1), swap(across, LO), swap(head, CORE), weight)
    from_left, from_right, across, head_other, weight = lax.optimization_barrier(first)
    left, right = call(ends_kernel, [states(1)] * 2, [VMEM], across)
    far_left, far_right = along(right, 1), along(left, -1)
    pack = functools.partial(pack_kernel, 5)
    middle = call(pack, states(12), [VMEM] * 5, tail, near, from_left, from_right, across)
    payload = ((8, 400, 128), BF, pltpu.VMEM)
    partial = call(
        early_kernel,
        payload,
        [VMEM] * 6,
        head,
        middle,
        head_other,
        swap(middle, CORE),
        weight,
        gain,
        flops=2 * 224 * 6144 * 512,
        scratch=[pltpu.VMEM((224, HALF), BF)],
    )
    pack = functools.partial(pack_kernel, 2)
    last = call(pack, states(2), [VMEM, VMEM, ANY], far_left, far_right, partial)
    partial = call(
        last_kernel,
        payload,
        [VMEM] * 5,
        partial,
        last,
        swap(last, CORE),
        weight,
        gain,
        flops=2 * 32 * 6144 * 512,
        scratch=[pltpu.VMEM((32, HALF), BF)],
        alias={0: 0},
    )
    partial = exchange(partial, (HI, X))
    joined = call(scale_kernel, ((8, 32, 512), BF, pltpu.VMEM), [VMEM], partial)
    return exchange(joined, (HI, X)).reshape(256, 512)


def solution(mesh):
    fine = Mesh(mesh.devices.reshape(4, 2, 2, 2, 4, 2), (ZQ, ZP, CORE, HI, X, LO))
    section, tensor = (ZQ, ZP, CORE), (HI, X)
    in_specs = (P(section, LO, tensor), P(), P(None, tensor), P(None, tensor, (*section, LO)))
    out_specs = P(None, (*section, LO))
    return jax.shard_map(shards, mesh=fine, in_specs=in_specs, out_specs=out_specs, check_vma=False)
```

time: 103 us -> 97.4 us (0.946)
  blocking collectives: 68.4 us -> 54.3 us
  waiting for transfers between devices: 7.16 us -> 13.5 us
    all_to_all x4 -> x3, blocking collectives: 68.4 us -> 54.3 us  [exchange(): return lax.all_to_all(a, axes, 0, 0, tiled=True)]
    ppermute x4 -> x7, waiting for transfers between devices: 1.76 us -> 10.9 us  [along(): return lax.ppermute(a, Z, [(i, (i + step) % 8) for i in range(8)])]
    ppermute x4 -> x7, starting transfers between devices: 4.21 us -> 9.79 us  [along(): return lax.ppermute(a, Z, [(i, (i + step) % 8) for i in range(8)])]
    ppermute x6, starting transfers between devices: 15.2 us -> 10.4 us  [swap(): return lax.ppermute(a, axis, [(0, 1), (1, 0)])]
    ppermute x6, waiting for transfers between devices: 5.4 us -> 2.62 us  [swap(): return lax.ppermute(a, axis, [(0, 1), (1, 0)])]
    pallas_call x9 -> x11, Pallas kernels: 7.44 us -> 8.39 us  [call(): pl.pallas_call(kernel, out_shape=[space(shape, kind) for shape, kind, spa...]
  transfers between devices with their start and end apart: 10 -> 13, of which waited for: 4 -> 7; matrix products, arithmetic and copies ran while one was open for 0% -> 0% of each run, Pallas kernels for 3% -> 5%
where the time goes in v4:
time: 97.4 us; the launch traced here: 97.2 us
  blocking collectives  54.3 us (56%)
  starting transfers between devices  20.2 us (21%)
  waiting for transfers between devices  13.5 us (14%)
  Pallas kernels  8.39 us (9%)
    all_to_all x3, blocking collectives, exchange(): return lax.all_to_all(a, axes, 0, 0, tiled=True)  54.3 us
    ppermute x7, waiting for transfers between devices, along(): return lax.ppermute(a, Z, [(i, (i + step) % 8) for i in range(8)])  10.9 us
    ppermute x6, starting transfers between devices, swap(): return lax.ppermute(a, axis, [(0, 1), (1, 0)])  10.4 us
    ppermute x7, starting transfers between devices, along(): return lax.ppermute(a, Z, [(i, (i + step) % 8) for i in range(8)])  9.79 us
    pallas_call x11, Pallas kernels, call(): pl.pallas_call(kernel, out_shape=[space(shape, kind) for shape, kind, spa...  8.39 us
    ppermute x6, waiting for transfers between devices, swap(): return lax.ppermute(a, axis, [(0, 1), (1, 0)])  2.62 us
  transfers between devices with their start and end apart: 13, of which 7 were waited for; matrix products, arithmetic and copies ran while one was open for 0% of the time, Pallas kernels for 5%

profile of v4, /device:TPU:1, one launch (start us, length us, event | category | flops | bytes accessed | tf_op | source)
XLA Modules:
  0.0 97.2 jit_solution(5070752515326494935)
XLA Ops:
  0.0 1.3 %shard_map.46 = (bf16[2,128,1024]{2,1,0:T(8,128)(2,1)S(1)}, bf16[2,128,1024]{2,1,0:T(8,128)(2,1)S(1)}, s32[3]{0:T(128)S(4)}, f32[3,2048]{1,0:T(4,128)S(1)}, s32[1]{0:T(128)S(4)}) custom-call(s32[3]{0:T(128)} %tap_hbm.1, bf16[2,128,2048]{2,1,0:T(8,128)(2,1)} %delta_hbm.1, f32[3,2048]{1,0:T(4,128)} %gain_hbm.1), custom_call_target="tpu_custom_call" | custom-call | bytes 1073164 | tf_op jit(solution)/shard_map/pallas_call | solution.py:29
  1.3 3.3 %collective-permute-start = (bf16[2,128,1024]{2,1,0:T(8,128)(2,1)S(1)}, bf16[2,128,1024]{2,1,0:T(8,128)(2,1)S(1)}, u32[]{:S(2)}, u32[]{:S(2)}) collective-permute-start(bf16[2,128,1024]{2,1,0:T(8,128)(2,1)S(1)} %get-tuple-element.31), channel_id=1, source_target_pairs={{0,16},{16,0},{1,17},{17,1},{2,18},{18,2},{3,19},{19,3},{4,20},{20... | collective-permute-start | bytes 1572872 | tf_op jit(solution)/shard_map/ppermute | solution.py:214
  4.6 1.5 %collective-permute-done.other_ref = bf16[2,128,1024]{2,1,0:T(8,128)(2,1)S(1)} collective-permute-done((bf16[2,128,1024]{2,1,0:T(8,128)(2,1)S(1)}, bf16[2,128,1024]{2,1,0:T(8,128)(2,1)S(1)}, u32[]{:S(2)}, u32[]{:S(2)}) %collective-permute-start) | collective-permute-done | bytes 524320 | tf_op jit(solution)/shard_map/ppermute | solution.py:214
  6.1 0.5 shard_map.47
  6.6 22.9 %all_to_all.20.ends_ref = bf16[8,2,16,1024]{3,2,1,0:T(8,128)(2,1)S(1)} all-to-all(bf16[8,2,16,1024]{3,2,1,0:T(8,128)(2,1)S(1)} %get-tuple-element.32), channel_id=1, replica_groups=mesh['zq'=4,'zp'=2,'core'=2,'hi'=2,'x'=4,'lo'=2] {'zq','zp'}, dimensions={0} | all-to-all | bytes 1048576 | tf_op jit(solution)/shard_map/all_to_all | solution.py:222
  29.6 0.4 shard_map.48.piece
  29.9 1.4 %collective-permute-start.4 = (bf16[1,3,16,1024]{3,2,1,0:T(8,128)(2,1)S(1)}, bf16[1,3,16,1024]{3,2,1,0:T(8,128)(2,1)S(1)}, u32[]{:S(2)}, u32[]{:S(2)}) collective-permute-start(bf16[1,3,16,1024]{3,2,1,0:T(8,128)(2,1)S(1)} %shard_map.48.piece), channel_id=1, source_target_pairs={{0,1},{1,0},{2,3},{3,2},{4,5},{5,4},{6,7},{7,6},{8,9},{9,8},{10,11... | collective-permute-start | bytes 294920 | tf_op jit(solution)/shard_map/ppermute | solution.py:214
  31.3 0.6 collective-permute-start.3
  31.9 1.7 %collective-permute-start.2 = (bf16[1,3,16,1024]{3,2,1,0:T(8,128)(2,1)S(1)}, bf16[1,3,16,1024]{3,2,1,0:T(8,128)(2,1)S(1)}, u32[]{:S(2)}, u32[]{:S(2)}) collective-permute-start(bf16[1,3,16,1024]{3,2,1,0:T(8,128)(2,1)S(1)} %shard_map.48.piece), channel_id=1, source_target_pairs={{0,192},{32,224},{64,0},{96,32},{128,64},{160,96},{192,128},{224,1... | collective-permute-start | bytes 294920 | tf_op jit(solution)/shard_map/ppermute | solution.py:218
  33.6 0.7 collective-permute-start.1
  34.3 0.0 collective-permute-done.4.near.refs_1_
  34.3 4.6 %collective-permute-done.3.far = bf16[1,3,16,1024]{3,2,1,0:T(8,128)(2,1)S(1)} collective-permute-done((bf16[1,3,16,1024]{3,2,1,0:T(8,128)(2,1)S(1)}, bf16[1,3,16,1024]{3,2,1,0:T(8,128)(2,1)S(1)}, u32[]{:S(2)}, u32[]{:S(2)}) %collective-permute-start.3) | collective-permute-done | bytes 98336 | tf_op jit(solution)/shard_map/ppermute | solution.py:218
  38.9 3.4 %collective-permute-done.2.above = bf16[1,3,16,1024]{3,2,1,0:T(8,128)(2,1)S(1)} collective-permute-done((bf16[1,3,16,1024]{3,2,1,0:T(8,128)(2,1)S(1)}, bf16[1,3,16,1024]{3,2,1,0:T(8,128)(2,1)S(1)}, u32[]{:S(2)}, u32[]{:S(2)}) %collective-permute-start.2) | collective-permute-done | bytes 98336 | tf_op jit(solution)/shard_map/ppermute | solution.py:218
  42.2 0.0 collective-permute-done.1.below
  42.2 0.1 shard_map.49
  42.3 3.9 %collective-permute-start.5 = (bf16[3,3,16,1024]{3,2,1,0:T(8,128)(2,1)S(1)}, bf16[3,3,16,1024]{3,2,1,0:T(8,128)(2,1)S(1)}, u32[]{:S(2)}, u32[]{:S(2)}) collective-permute-start(bf16[3,3,16,1024]{3,2,1,0:T(8,128)(2,1)S(1)} %get-tuple-element.38), channel_id=1, source_target_pairs={{0,32},{32,64},{64,96},{96,128},{128,160},{160,192},{192,224},{224... | collective-permute-start | bytes 884744 | tf_op jit(solution)/shard_map/ppermute | solution.py:218
  46.3 0.2 collective-permute-start.6
  46.4 0.2 collective-permute-start.7
  46.6 2.3 %collective-permute-start.8 = (bf16[2,3,16,1024]{3,2,1,0:T(8,128)(2,1)S(1)}, bf16[2,3,16,1024]{3,2,1,0:T(8,128)(2,1)S(1)}, u32[]{:S(2)}, u32[]{:S(2)}) collective-permute-start(bf16[2,3,16,1024]{3,2,1,0:T(8,128)(2,1)S(1)} %get-tuple-element.36.head), channel_id=1, source_target_pairs={{0,16},{16,0},{1,17},{17,1},{2,18},{18,2},{3,19},{19,3},{4,20},{20... | collective-permute-start | bytes 589832 | tf_op jit(solution)/shard_map/ppermute | solution.py:214
  48.9 2.8 %shard_map.50.weight_ref = bf16[3,2048,512]{2,1,0:T(8,128)(2,1)S(1)} custom-call(bf16[3,2048,512]{2,1,0:T(8,128)(2,1)} %weight_hbm.1, bf16[3,3,16,1024]{3,2,1,0:T(8,128)(2,1)S(1)} %get-tuple-element.40.after_ref), custom_call_target="tpu_custom_call" | custom-call | bytes 6586368 | tf_op jit(solution)/shard_map/pallas_call | solution.py:29
  51.7 0.0 collective-permute-done.8.head_other
  51.7 0.2 collective-permute-done.5.refs_2_
  51.9 1.8 %collective-permute-done.6.refs_3_ = bf16[3,3,16,1024]{3,2,1,0:T(8,128)(2,1)S(1)} collective-permute-done((bf16[3,3,16,1024]{3,2,1,0:T(8,128)(2,1)S(1)}, bf16[3,3,16,1024]{3,2,1,0:T(8,128)(2,1)S(1)}, u32[]{:S(2)}, u32[]{:S(2)}) %collective-permute-start.6) | collective-permute-done | bytes 294944 | tf_op jit(solution)/shard_map/ppermute | solution.py:218
  53.7 0.0 collective-permute-done.7.refs_4_.across_ref
  53.7 0.1 shard_map.51.middle
  53.7 2.3 %collective-permute-start.9 = (bf16[12,3,16,1024]{3,2,1,0:T(8,128)(2,1)S(1)}, bf16[12,3,16,1024]{3,2,1,0:T(8,128)(2,1)S(1)}, u32[]{:S(2)}, u32[]{:S(2)}) collective-permute-start(bf16[12,3,16,1024]{3,2,1,0:T(8,128)(2,1)S(1)} %shard_map.51.middle), channel_id=1, source_target_pairs={{0,16},{16,0},{1,17},{17,1},{2,18},{18,2},{3,19},{19,3},{4,20},{20... | collective-permute-start | bytes 3538952 | tf_op jit(solution)/shard_map/ppermute | solution.py:214
  56.0 1.4 %collective-permute-start.10 = (bf16[1,3,16,1024]{3,2,1,0:T(8,128)(2,1)S(1)}, bf16[1,3,16,1024]{3,2,1,0:T(8,128)(2,1)S(1)}, u32[]{:S(2)}, u32[]{:S(2)}) collective-permute-start(bf16[1,3,16,1024]{3,2,1,0:T(8,128)(2,1)S(1)} %get-tuple-element.46), channel_id=1, source_target_pairs={{0,32},{32,64},{64,96},{96,128},{128,160},{160,192},{192,224},{224... | collective-permute-start | bytes 294920 | tf_op jit(solution)/shard_map/ppermute | solution.py:218
  57.4 1.4 %collective-permute-start.11 = (bf16[1,3,16,1024]{3,2,1,0:T(8,128)(2,1)S(1)}, bf16[1,3,16,1024]{3,2,1,0:T(8,128)(2,1)S(1)}, u32[]{:S(2)}, u32[]{:S(2)}) collective-permute-start(bf16[1,3,16,1024]{3,2,1,0:T(8,128)(2,1)S(1)} %get-tuple-element.47), channel_id=1, source_target_pairs={{0,224},{32,0},{64,32},{96,64},{128,96},{160,128},{192,160},{224,1... | collective-permute-start | bytes 294920 | tf_op jit(solution)/shard_map/ppermute | solution.py:218
  58.8 0.0 collective-permute-done.9.middle_other
  58.8 2.0 %shard_map.52.refs_2_.early_ref = bf16[8,400,128]{2,1,0:T(8,128)(2,1)S(1)} custom-call(bf16[2,3,16,1024]{3,2,1,0:T(8,128)(2,1)S(1)} %get-tuple-element.36.head, bf16[12,3,16,1024]{3,2,1,0:T(8,128)(2,1)S(1)} %shard_map.51.middle, bf16[2,3,16,1024]{3,2,1,0:T(8,128)(2,1)S(1)} %collective-permute-done.8.head_other, ...), custom_call_target="tpu_custom_call" | custom-call | flops 1409286144 | bytes 9068544 | tf_op jit(solution)/shard_map/pallas_call | solution.py:29
  60.8 0.9 collective-permute-done.10.refs_0_
  61.7 0.0 collective-permute-done.11.refs_1_
  61.8 1.0 %collective-permute-start.12 = (bf16[2,3,16,1024]{3,2,1,0:T(8,128)(2,1)S(1)}, bf16[2,3,16,1024]{3,2,1,0:T(8,128)(2,1)S(1)}, u32[]{:S(2)}, u32[]{:S(2)}) collective-permute-start(bf16[2,3,16,1024]{3,2,1,0:T(8,128)(2,1)S(1)} %shard_map.54.last), channel_id=1, source_target_pairs={{0,16},{16,0},{1,17},{17,1},{2,18},{18,2},{3,19},{19,3},{4,20},{20... | collective-permute-start | bytes 589832 | tf_op jit(solution)/shard_map/ppermute | solution.py:214
  62.7 1.1 %collective-permute-done.12.last_other = bf16[2,3,16,1024]{3,2,1,0:T(8,128)(2,1)S(1)} collective-permute-done((bf16[2,3,16,1024]{3,2,1,0:T(8,128)(2,1)S(1)}, bf16[2,3,16,1024]{3,2,1,0:T(8,128)(2,1)S(1)}, u32[]{:S(2)}, u32[]{:S(2)}) %collective-permute-start.12) | collective-permute-done | bytes 196640 | tf_op jit(solution)/shard_map/ppermute | solution.py:214
  63.8 1.2 %shard_map.55 = bf16[8,400,128]{2,1,0:T(8,128)(2,1)S(1)} custom-call(bf16[8,400,128]{2,1,0:T(8,128)(2,1)S(1)} %shard_map.52.refs_2_.early_ref, bf16[2,3,16,1024]{3,2,1,0:T(8,128)(2,1)S(1)} %shard_map.54.last, bf16[2,3,16,1024]{3,2,1,0:T(8,128)(2,1)S(1)} %collective-permute-done.12.last_other, ...), custom_call_target="tpu_custom_call", output_to_operand_aliasing={{}: (0, {})} | custom-call | flops 201326592 | bytes 7528448 | tf_op jit(solution)/shard_map/pallas_call | solution.py:29
  65.0 21.0 %all_to_all.21.parts_ref = bf16[8,400,128]{2,1,0:T(8,128)(2,1)S(1)} all-to-all(bf16[8,400,128]{2,1,0:T(8,128)(2,1)S(1)} %shard_map.55), channel_id=1, replica_groups=mesh['zq'=4,'zp'=2,'core'=2,'hi'=2,'x'=4,'lo'=2] {'hi','x'}, dimensions={0} | all-to-all | bytes 1638400 | tf_op jit(solution)/shard_map/all_to_all | solution.py:222
  86.0 0.1 shard_map.56
  86.1 10.4 %all_to_all.22 = bf16[8,32,512]{2,1,0:T(8,128)(2,1)S(1)} all-to-all(bf16[8,32,512]{2,1,0:T(8,128)(2,1)S(1)} %shard_map.56), channel_id=1, replica_groups=mesh['zq'=4,'zp'=2,'core'=2,'hi'=2,'x'=4,'lo'=2] {'hi','x'}, dimensions={0} | all-to-all | bytes 524288 | tf_op jit(solution)/shard_map/all_to_all | solution.py:222
  96.5 0.7 copy.11
  (3 shorter events, 0.0 us)
Async XLA Ops:
  1.3 4.9 %collective-permute-start = (bf16[2,128,1024]{2,1,0:T(8,128)(2,1)S(1)}, bf16[2,128,1024]{2,1,0:T(8,128)(2,1)S(1)}, u32[]{:S(2)}, u32[]{:S(2)}) collective-permute-start(bf16[2,128,1024]{2,1,0:T(8,128)(2,1)S(1)} %get-tuple-element.31), channel_id=1, source_target_pairs={{0,16},{16,0},{1,17},{17,1},{2,18},{18,2},{3,19},{19,3},{4,20},{20... | collective-permute-start | bytes 1572872 | tf_op jit(solution)/shard_map/ppermute | solution.py:214
  29.9 4.3 %collective-permute-start.4 = (bf16[1,3,16,1024]{3,2,1,0:T(8,128)(2,1)S(1)}, bf16[1,3,16,1024]{3,2,1,0:T(8,128)(2,1)S(1)}, u32[]{:S(2)}, u32[]{:S(2)}) collective-permute-start(bf16[1,3,16,1024]{3,2,1,0:T(8,128)(2,1)S(1)} %shard_map.48.piece), channel_id=1, source_target_pairs={{0,1},{1,0},{2,3},{3,2},{4,5},{5,4},{6,7},{7,6},{8,9},{9,8},{10,11... | collective-permute-start | bytes 294920 | tf_op jit(solution)/shard_map/ppermute | solution.py:214
  31.3 7.6 %collective-permute-start.3 = (bf16[1,3,16,1024]{3,2,1,0:T(8,128)(2,1)S(1)}, bf16[1,3,16,1024]{3,2,1,0:T(8,128)(2,1)S(1)}, u32[]{:S(2)}, u32[]{:S(2)}) collective-permute-start(bf16[1,3,16,1024]{3,2,1,0:T(8,128)(2,1)S(1)} %shard_map.48.piece), channel_id=1, source_target_pairs={{0,128},{32,160},{64,192},{96,224},{128,0},{160,32},{192,64},{224,... | collective-permute-start | bytes 294920 | tf_op jit(solution)/shard_map/ppermute | solution.py:218
  31.9 10.3 %collective-permute-start.2 = (bf16[1,3,16,1024]{3,2,1,0:T(8,128)(2,1)S(1)}, bf16[1,3,16,1024]{3,2,1,0:T(8,128)(2,1)S(1)}, u32[]{:S(2)}, u32[]{:S(2)}) collective-permute-start(bf16[1,3,16,1024]{3,2,1,0:T(8,128)(2,1)S(1)} %shard_map.48.piece), channel_id=1, source_target_pairs={{0,192},{32,224},{64,0},{96,32},{128,64},{160,96},{192,128},{224,1... | collective-permute-start | bytes 294920 | tf_op jit(solution)/shard_map/ppermute | solution.py:218
  33.6 8.7 %collective-permute-start.1 = (bf16[1,3,16,1024]{3,2,1,0:T(8,128)(2,1)S(1)}, bf16[1,3,16,1024]{3,2,1,0:T(8,128)(2,1)S(1)}, u32[]{:S(2)}, u32[]{:S(2)}) collective-permute-start(bf16[1,3,16,1024]{3,2,1,0:T(8,128)(2,1)S(1)} %shard_map.48.piece), channel_id=1, source_target_pairs={{0,64},{32,96},{64,128},{96,160},{128,192},{160,224},{192,0},{224,... | collective-permute-start | bytes 294920 | tf_op jit(solution)/shard_map/ppermute | solution.py:218
  42.3 9.5 %collective-permute-start.5 = (bf16[3,3,16,1024]{3,2,1,0:T(8,128)(2,1)S(1)}, bf16[3,3,16,1024]{3,2,1,0:T(8,128)(2,1)S(1)}, u32[]{:S(2)}, u32[]{:S(2)}) collective-permute-start(bf16[3,3,16,1024]{3,2,1,0:T(8,128)(2,1)S(1)} %get-tuple-element.38), channel_id=1, source_target_pairs={{0,32},{32,64},{64,96},{96,128},{128,160},{160,192},{192,224},{224... | collective-permute-start | bytes 884744 | tf_op jit(solution)/shard_map/ppermute | solution.py:218
  46.3 7.4 %collective-permute-start.6 = (bf16[3,3,16,1024]{3,2,1,0:T(8,128)(2,1)S(1)}, bf16[3,3,16,1024]{3,2,1,0:T(8,128)(2,1)S(1)}, u32[]{:S(2)}, u32[]{:S(2)}) collective-permute-start(bf16[3,3,16,1024]{3,2,1,0:T(8,128)(2,1)S(1)} %get-tuple-element.39), channel_id=1, source_target_pairs={{0,224},{32,0},{64,32},{96,64},{128,96},{160,128},{192,160},{224,1... | collective-permute-start | bytes 884744 | tf_op jit(solution)/shard_map/ppermute | solution.py:218
  46.4 7.2 %collective-permute-start.7 = (bf16[3,3,16,1024]{3,2,1,0:T(8,128)(2,1)S(1)}, bf16[3,3,16,1024]{3,2,1,0:T(8,128)(2,1)S(1)}, u32[]{:S(2)}, u32[]{:S(2)}) collective-permute-start(bf16[3,3,16,1024]{3,2,1,0:T(8,128)(2,1)S(1)} %get-tuple-element.40.after_ref), channel_id=1, source_target_pairs={{0,1},{1,0},{2,3},{3,2},{4,5},{5,4},{6,7},{7,6},{8,9},{9,8},{10,11... | collective-permute-start | bytes 884744 | tf_op jit(solution)/shard_map/ppermute | solution.py:214
  46.6 5.1 %collective-permute-start.8 = (bf16[2,3,16,1024]{3,2,1,0:T(8,128)(2,1)S(1)}, bf16[2,3,16,1024]{3,2,1,0:T(8,128)(2,1)S(1)}, u32[]{:S(2)}, u32[]{:S(2)}) collective-permute-start(bf16[2,3,16,1024]{3,2,1,0:T(8,128)(2,1)S(1)} %get-tuple-element.36.head), channel_id=1, source_target_pairs={{0,16},{16,0},{1,17},{17,1},{2,18},{18,2},{3,19},{19,3},{4,20},{20... | collective-permute-start | bytes 589832 | tf_op jit(solution)/shard_map/ppermute | solution.py:214
  53.7 5.0 %collective-permute-start.9 = (bf16[12,3,16,1024]{3,2,1,0:T(8,128)(2,1)S(1)}, bf16[12,3,16,1024]{3,2,1,0:T(8,128)(2,1)S(1)}, u32[]{:S(2)}, u32[]{:S(2)}) collective-permute-start(bf16[12,3,16,1024]{3,2,1,0:T(8,128)(2,1)S(1)} %shard_map.51.middle), channel_id=1, source_target_pairs={{0,16},{16,0},{1,17},{17,1},{2,18},{18,2},{3,19},{19,3},{4,20},{20... | collective-permute-start | bytes 3538952 | tf_op jit(solution)/shard_map/ppermute | solution.py:214
  56.0 5.7 %collective-permute-start.10 = (bf16[1,3,16,1024]{3,2,1,0:T(8,128)(2,1)S(1)}, bf16[1,3,16,1024]{3,2,1,0:T(8,128)(2,1)S(1)}, u32[]{:S(2)}, u32[]{:S(2)}) collective-permute-start(bf16[1,3,16,1024]{3,2,1,0:T(8,128)(2,1)S(1)} %get-tuple-element.46), channel_id=1, source_target_pairs={{0,32},{32,64},{64,96},{96,128},{128,160},{160,192},{192,224},{224... | collective-permute-start | bytes 294920 | tf_op jit(solution)/shard_map/ppermute | solution.py:218
  57.4 4.3 %collective-permute-start.11 = (bf16[1,3,16,1024]{3,2,1,0:T(8,128)(2,1)S(1)}, bf16[1,3,16,1024]{3,2,1,0:T(8,128)(2,1)S(1)}, u32[]{:S(2)}, u32[]{:S(2)}) collective-permute-start(bf16[1,3,16,1024]{3,2,1,0:T(8,128)(2,1)S(1)} %get-tuple-element.47), channel_id=1, source_target_pairs={{0,224},{32,0},{64,32},{96,64},{128,96},{160,128},{192,160},{224,1... | collective-permute-start | bytes 294920 | tf_op jit(solution)/shard_map/ppermute | solution.py:218
  61.8 2.0 %collective-permute-start.12 = (bf16[2,3,16,1024]{3,2,1,0:T(8,128)(2,1)S(1)}, bf16[2,3,16,1024]{3,2,1,0:T(8,128)(2,1)S(1)}, u32[]{:S(2)}, u32[]{:S(2)}) collective-permute-start(bf16[2,3,16,1024]{3,2,1,0:T(8,128)(2,1)S(1)} %shard_map.54.last), channel_id=1, source_target_pairs={{0,16},{16,0},{1,17},{17,1},{2,18},{18,2},{3,19},{19,3},{4,20},{20... | collective-permute-start | bytes 589832 | tf_op jit(solution)/shard_map/ppermute | solution.py:214

commit v5 on v4

--- a/solution.py
+++ b/solution.py
@@ -110,18 +110,6 @@
     early += [mine + lax.rem(z + 1, 8), mine + lax.rem(z + 3, 8), yours + lax.rem(z + 1, 8)]
     early += [yours + lax.rem(z + step, 8) for step in (2, 6, 4)]
     return early, [yours + lax.rem(z + 5, 8), yours + lax.rem(z + 3, 8)]
-
-
-def cut_kernel(piece, below, above, far, near, right_ref, left_ref, across_ref, head_ref, tail_ref):
-    for out_ref, refs in (
-        (right_ref, (piece, below, near)),
-        (left_ref, (piece, above, near)),
-        (across_ref, (above, below, far)),
-        (head_ref, (piece, below)),
-        (tail_ref, (above, far)),
-    ):
-        for i, ref in enumerate(refs):
-            out_ref[i] = ref[0]
 
 
 def pack_kernel(count, *refs):
@@ -256,8 +244,13 @@
     far = along(piece, 4)
     below, above = along(piece, 2), along(piece, -2)
     near = swap(piece, LO)
-    parts = [states(3)] * 3 + [states(2)] * 2
-    right, left, across, head, tail = call(cut_kernel, parts, [VMEM] * 5, piece, below, above, far, near)
+    pack = functools.partial(pack_kernel, 3)
+    across = call(pack, states(3), [VMEM] * 3, above, below, far)
+    right = call(pack, states(3), [VMEM] * 3, piece, below, near)
+    left = call(pack, states(3), [VMEM] * 3, piece, above, near)
+    pack = functools.partial(pack_kernel, 2)
+    head = call(pack, states(2), [VMEM] * 2, piece, below)
+    tail = call(pack, states(2), [VMEM] * 2, above, far)
     weight = call(
         fetch_kernel,
         (fc_weight.shape, BF, pltpu.VMEM),
@@ -266,8 +259,8 @@
         across,
         scratch=[pltpu.SemaphoreType.DMA],
     )
-    first = (along(right, 1), along(left, -1), swap(across, LO), swap(head, CORE), weight)
-    from_left, from_right, across, head_other, weight = lax.optimization_barrier(first)
+    first = (swap(across, LO), along(right, 1), along(left, -1), swap(head, CORE), weight)
+    across, from_left, from_right, head_other, weight = lax.optimization_barrier(first)
     left, right = call(ends_kernel, [states(1)] * 2, [VMEM], across)
     far_left, far_right = along(right, 1), along(left, -1)
     pack = functools.partial(pack_kernel, 5)
@@ -301,9 +294,9 @@
         scratch=[pltpu.VMEM((32, HALF), BF)],
         alias={0: 0},
     )
-    partial = exchange(partial, (HI, X))
+    partial = exchange(partial, (X, HI))
     joined = call(scale_kernel, ((8, 32, 512), BF, pltpu.VMEM), [VMEM], partial)
-    return exchange(joined, (HI, X)).reshape(256, 512)
+    return exchange(joined, (X, HI)).reshape(256, 512)
 
 
 def solution(mesh):

time: 97.4 us -> 94.4 us (0.969)
  waiting for transfers between devices: 13.5 us -> 8.77 us
  starting transfers between devices: 20.2 us -> 23.1 us
  blocking collectives: 54.3 us -> 53.1 us
    ppermute x6, starting transfers between devices: 10.4 us -> 15.5 us  [swap(): return lax.ppermute(a, axis, [(0, 1), (1, 0)])]
    ppermute x7, waiting for transfers between devices: 10.9 us -> 6.15 us  [along(): return lax.ppermute(a, Z, [(i, (i + step) % 8) for i in range(8)])]
    ppermute x7, starting transfers between devices: 9.79 us -> 7.6 us  [along(): return lax.ppermute(a, Z, [(i, (i + step) % 8) for i in range(8)])]
    all_to_all x3, blocking collectives: 54.3 us -> 53.1 us  [exchange(): return lax.all_to_all(a, axes, 0, 0, tiled=True)]
    pallas_call x11 -> x15, Pallas kernels: 8.39 us -> 8.39 us  [call(): pl.pallas_call(kernel, out_shape=[space(shape, kind) for shape, kind, spa...]
  transfers between devices with their start and end apart: 13 -> 13, of which waited for: 7 -> 6; matrix products, arithmetic and copies ran while one was open for 0% -> 0% of each run, Pallas kernels for 5% -> 5%
where the time goes in v5:
time: 94.4 us; the launch traced here: 94.2 us
  blocking collectives  53.1 us (56%)
  starting transfers between devices  23.1 us (24%)
  waiting for transfers between devices  8.77 us (9%)
  Pallas kernels  8.39 us (9%)
    all_to_all x3, blocking collectives, exchange(): return lax.all_to_all(a, axes, 0, 0, tiled=True)  53.1 us
    ppermute x6, starting transfers between devices, swap(): return lax.ppermute(a, axis, [(0, 1), (1, 0)])  15.5 us
    pallas_call x15, Pallas kernels, call(): pl.pallas_call(kernel, out_shape=[space(shape, kind) for shape, kind, spa...  8.39 us
    ppermute x7, starting transfers between devices, along(): return lax.ppermute(a, Z, [(i, (i + step) % 8) for i in range(8)])  7.6 us
    ppermute x7, waiting for transfers between devices, along(): return lax.ppermute(a, Z, [(i, (i + step) % 8) for i in range(8)])  6.15 us
    ppermute x6, waiting for transfers between devices, swap(): return lax.ppermute(a, axis, [(0, 1), (1, 0)])  2.62 us
  transfers between devices with their start and end apart: 13, of which 6 were waited for; matrix products, arithmetic and copies ran while one was open for 0% of the time, Pallas kernels for 5%

profile of v5, /device:TPU:1, one launch (start us, length us, event | category | flops | bytes accessed | tf_op | source)
XLA Modules:
  0.0 94.2 jit_solution(3524962021506649436)
XLA Ops:
  0.0 1.3 %shard_map.46 = (bf16[2,128,1024]{2,1,0:T(8,128)(2,1)S(1)}, bf16[2,128,1024]{2,1,0:T(8,128)(2,1)S(1)}, s32[3]{0:T(128)S(4)}, f32[3,2048]{1,0:T(4,128)S(1)}, s32[1]{0:T(128)S(4)}) custom-call(s32[3]{0:T(128)} %tap_hbm.1, bf16[2,128,2048]{2,1,0:T(8,128)(2,1)} %delta_hbm.1, f32[3,2048]{1,0:T(4,128)} %gain_hbm.1), custom_call_target="tpu_custom_call" | custom-call | bytes 1073164 | tf_op jit(solution)/shard_map/pallas_call | solution.py:29
  1.3 3.3 %collective-permute-start = (bf16[2,128,1024]{2,1,0:T(8,128)(2,1)S(1)}, bf16[2,128,1024]{2,1,0:T(8,128)(2,1)S(1)}, u32[]{:S(2)}, u32[]{:S(2)}) collective-permute-start(bf16[2,128,1024]{2,1,0:T(8,128)(2,1)S(1)} %get-tuple-element.26), channel_id=1, source_target_pairs={{0,16},{16,0},{1,17},{17,1},{2,18},{18,2},{3,19},{19,3},{4,20},{20... | collective-permute-start | bytes 1572872 | tf_op jit(solution)/shard_map/ppermute | solution.py:202
  4.6 1.5 %collective-permute-done.other_ref = bf16[2,128,1024]{2,1,0:T(8,128)(2,1)S(1)} collective-permute-done((bf16[2,128,1024]{2,1,0:T(8,128)(2,1)S(1)}, bf16[2,128,1024]{2,1,0:T(8,128)(2,1)S(1)}, u32[]{:S(2)}, u32[]{:S(2)}) %collective-permute-start) | collective-permute-done | bytes 524320 | tf_op jit(solution)/shard_map/ppermute | solution.py:202
  6.1 0.5 shard_map.47
  6.6 22.9 %all_to_all.20.ends_ref = bf16[8,2,16,1024]{3,2,1,0:T(8,128)(2,1)S(1)} all-to-all(bf16[8,2,16,1024]{3,2,1,0:T(8,128)(2,1)S(1)} %get-tuple-element.27), channel_id=1, replica_groups=mesh['zq'=4,'zp'=2,'core'=2,'hi'=2,'x'=4,'lo'=2] {'zq','zp'}, dimensions={0} | all-to-all | bytes 1048576 | tf_op jit(solution)/shard_map/all_to_all | solution.py:210
  29.6 0.4 shard_map.48.refs_0_
  29.9 1.4 %collective-permute-start.4 = (bf16[1,3,16,1024]{3,2,1,0:T(8,128)(2,1)S(1)}, bf16[1,3,16,1024]{3,2,1,0:T(8,128)(2,1)S(1)}, u32[]{:S(2)}, u32[]{:S(2)}) collective-permute-start(bf16[1,3,16,1024]{3,2,1,0:T(8,128)(2,1)S(1)} %shard_map.48.refs_0_), channel_id=1, source_target_pairs={{0,1},{1,0},{2,3},{3,2},{4,5},{5,4},{6,7},{7,6},{8,9},{9,8},{10,11... | collective-permute-start | bytes 294920 | tf_op jit(solution)/shard_map/ppermute | solution.py:202
  31.3 0.7 collective-permute-start.2
  32.0 1.7 %collective-permute-start.1 = (bf16[1,3,16,1024]{3,2,1,0:T(8,128)(2,1)S(1)}, bf16[1,3,16,1024]{3,2,1,0:T(8,128)(2,1)S(1)}, u32[]{:S(2)}, u32[]{:S(2)}) collective-permute-start(bf16[1,3,16,1024]{3,2,1,0:T(8,128)(2,1)S(1)} %shard_map.48.refs_0_), channel_id=1, source_target_pairs={{0,64},{32,96},{64,128},{96,160},{128,192},{160,224},{192,0},{224,... | collective-permute-start | bytes 294920 | tf_op jit(solution)/shard_map/ppermute | solution.py:206
  33.7 0.6 collective-permute-start.3
  34.3 0.0 collective-permute-done.4.refs_2_.refs_1_
  34.3 1.5 %collective-permute-done.2.refs_0_.refs_1_ = bf16[1,3,16,1024]{3,2,1,0:T(8,128)(2,1)S(1)} collective-permute-done((bf16[1,3,16,1024]{3,2,1,0:T(8,128)(2,1)S(1)}, bf16[1,3,16,1024]{3,2,1,0:T(8,128)(2,1)S(1)}, u32[]{:S(2)}, u32[]{:S(2)}) %collective-permute-start.2) | collective-permute-done | bytes 98336 | tf_op jit(solution)/shard_map/ppermute | solution.py:206
  35.8 1.8 %collective-permute-start.7 = (bf16[3,3,16,1024]{3,2,1,0:T(8,128)(2,1)S(1)}, bf16[3,3,16,1024]{3,2,1,0:T(8,128)(2,1)S(1)}, u32[]{:S(2)}, u32[]{:S(2)}) collective-permute-start(bf16[3,3,16,1024]{3,2,1,0:T(8,128)(2,1)S(1)} %shard_map.53), channel_id=1, source_target_pairs={{0,224},{32,0},{64,32},{96,64},{128,96},{160,128},{192,160},{224,1... | collective-permute-start | bytes 884744 | tf_op jit(solution)/shard_map/ppermute | solution.py:206
  37.6 0.5 collective-permute-done.1.refs_1_
  38.2 0.1 collective-permute-start.6
  38.3 3.2 %collective-permute-done.3.refs_1_.refs_2_ = bf16[1,3,16,1024]{3,2,1,0:T(8,128)(2,1)S(1)} collective-permute-done((bf16[1,3,16,1024]{3,2,1,0:T(8,128)(2,1)S(1)}, bf16[1,3,16,1024]{3,2,1,0:T(8,128)(2,1)S(1)}, u32[]{:S(2)}, u32[]{:S(2)}) %collective-permute-start.3) | collective-permute-done | bytes 98336 | tf_op jit(solution)/shard_map/ppermute | solution.py:206
  41.5 0.3 collective-permute-start.5
  41.7 6.3 %collective-permute-start.8 = (bf16[2,3,16,1024]{3,2,1,0:T(8,128)(2,1)S(1)}, bf16[2,3,16,1024]{3,2,1,0:T(8,128)(2,1)S(1)}, u32[]{:S(2)}, u32[]{:S(2)}) collective-permute-start(bf16[2,3,16,1024]{3,2,1,0:T(8,128)(2,1)S(1)} %shard_map.49.head), channel_id=1, source_target_pairs={{0,16},{16,0},{1,17},{17,1},{2,18},{18,2},{3,19},{19,3},{4,20},{20... | collective-permute-start | bytes 589832 | tf_op jit(solution)/shard_map/ppermute | solution.py:202
  48.0 2.8 %shard_map.54.weight_ref = bf16[3,2048,512]{2,1,0:T(8,128)(2,1)S(1)} custom-call(bf16[3,2048,512]{2,1,0:T(8,128)(2,1)} %weight_hbm.1, bf16[3,3,16,1024]{3,2,1,0:T(8,128)(2,1)S(1)} %shard_map.51.after_ref), custom_call_target="tpu_custom_call" | custom-call | bytes 6586368 | tf_op jit(solution)/shard_map/pallas_call | solution.py:29
  50.8 0.0 collective-permute-done.8.head_other
  50.8 0.0 collective-permute-done.7.refs_3_
  50.8 0.0 collective-permute-done.6.refs_2_
  50.8 0.0 collective-permute-done.5.refs_4_.across_ref
  50.9 0.1 shard_map.55.middle
  50.9 3.4 %collective-permute-start.9 = (bf16[12,3,16,1024]{3,2,1,0:T(8,128)(2,1)S(1)}, bf16[12,3,16,1024]{3,2,1,0:T(8,128)(2,1)S(1)}, u32[]{:S(2)}, u32[]{:S(2)}) collective-permute-start(bf16[12,3,16,1024]{3,2,1,0:T(8,128)(2,1)S(1)} %shard_map.55.middle), channel_id=1, source_target_pairs={{0,16},{16,0},{1,17},{17,1},{2,18},{18,2},{3,19},{19,3},{4,20},{20... | collective-permute-start | bytes 3538952 | tf_op jit(solution)/shard_map/ppermute | solution.py:202
  54.3 0.1 collective-permute-start.10
  54.4 2.7 %collective-permute-start.11 = (bf16[1,3,16,1024]{3,2,1,0:T(8,128)(2,1)S(1)}, bf16[1,3,16,1024]{3,2,1,0:T(8,128)(2,1)S(1)}, u32[]{:S(2)}, u32[]{:S(2)}) collective-permute-start(bf16[1,3,16,1024]{3,2,1,0:T(8,128)(2,1)S(1)} %get-tuple-element.37), channel_id=1, source_target_pairs={{0,224},{32,0},{64,32},{96,64},{128,96},{160,128},{192,160},{224,1... | collective-permute-start | bytes 294920 | tf_op jit(solution)/shard_map/ppermute | solution.py:206
  57.1 0.0 collective-permute-done.9.middle_other
  57.1 2.0 %shard_map.56.refs_2_.early_ref = bf16[8,400,128]{2,1,0:T(8,128)(2,1)S(1)} custom-call(bf16[2,3,16,1024]{3,2,1,0:T(8,128)(2,1)S(1)} %shard_map.49.head, bf16[12,3,16,1024]{3,2,1,0:T(8,128)(2,1)S(1)} %shard_map.55.middle, bf16[2,3,16,1024]{3,2,1,0:T(8,128)(2,1)S(1)} %collective-permute-done.8.head_other, ...), custom_call_target="tpu_custom_call" | custom-call | flops 1409286144 | bytes 9068544 | tf_op jit(solution)/shard_map/pallas_call | solution.py:29
  59.1 0.9 collective-permute-done.10.refs_0_
  60.0 0.0 collective-permute-done.11.refs_1_
  60.1 0.9 collective-permute-start.12
  61.0 1.1 %collective-permute-done.12.last_other = bf16[2,3,16,1024]{3,2,1,0:T(8,128)(2,1)S(1)} collective-permute-done((bf16[2,3,16,1024]{3,2,1,0:T(8,128)(2,1)S(1)}, bf16[2,3,16,1024]{3,2,1,0:T(8,128)(2,1)S(1)}, u32[]{:S(2)}, u32[]{:S(2)}) %collective-permute-start.12) | collective-permute-done | bytes 196640 | tf_op jit(solution)/shard_map/ppermute | solution.py:202
  62.0 1.2 %shard_map.59 = bf16[8,400,128]{2,1,0:T(8,128)(2,1)S(1)} custom-call(bf16[8,400,128]{2,1,0:T(8,128)(2,1)S(1)} %shard_map.56.refs_2_.early_ref, bf16[2,3,16,1024]{3,2,1,0:T(8,128)(2,1)S(1)} %shard_map.58.last, bf16[2,3,16,1024]{3,2,1,0:T(8,128)(2,1)S(1)} %collective-permute-done.12.last_other, ...), custom_call_target="tpu_custom_call", output_to_operand_aliasing={{}: (0, {})} | custom-call | flops 201326592 | bytes 7528448 | tf_op jit(solution)/shard_map/pallas_call | solution.py:29
  63.2 20.4 %all_to_all.21.parts_ref = bf16[8,400,128]{2,1,0:T(8,128)(2,1)S(1)} all-to-all(bf16[8,400,128]{2,1,0:T(8,128)(2,1)S(1)} %shard_map.59), channel_id=1, replica_groups=mesh['zq'=4,'zp'=2,'core'=2,'hi'=2,'x'=4,'lo'=2] {'x','hi'}, dimensions={0} | all-to-all | bytes 1638400 | tf_op jit(solution)/shard_map/all_to_all | solution.py:210
  83.6 0.1 shard_map.60
  83.7 9.8 %all_to_all.22 = bf16[8,32,512]{2,1,0:T(8,128)(2,1)S(1)} all-to-all(bf16[8,32,512]{2,1,0:T(8,128)(2,1)S(1)} %shard_map.60), channel_id=1, replica_groups=mesh['zq'=4,'zp'=2,'core'=2,'hi'=2,'x'=4,'lo'=2] {'x','hi'}, dimensions={0} | all-to-all | bytes 524288 | tf_op jit(solution)/shard_map/all_to_all | solution.py:210
  93.5 0.7 copy.11
  (8 shorter events, 0.1 us)
Async XLA Ops:
  1.3 4.9 %collective-permute-start = (bf16[2,128,1024]{2,1,0:T(8,128)(2,1)S(1)}, bf16[2,128,1024]{2,1,0:T(8,128)(2,1)S(1)}, u32[]{:S(2)}, u32[]{:S(2)}) collective-permute-start(bf16[2,128,1024]{2,1,0:T(8,128)(2,1)S(1)} %get-tuple-element.26), channel_id=1, source_target_pairs={{0,16},{16,0},{1,17},{17,1},{2,18},{18,2},{3,19},{19,3},{4,20},{20... | collective-permute-start | bytes 1572872 | tf_op jit(solution)/shard_map/ppermute | solution.py:202
  29.9 4.3 %collective-permute-start.4 = (bf16[1,3,16,1024]{3,2,1,0:T(8,128)(2,1)S(1)}, bf16[1,3,16,1024]{3,2,1,0:T(8,128)(2,1)S(1)}, u32[]{:S(2)}, u32[]{:S(2)}) collective-permute-start(bf16[1,3,16,1024]{3,2,1,0:T(8,128)(2,1)S(1)} %shard_map.48.refs_0_), channel_id=1, source_target_pairs={{0,1},{1,0},{2,3},{3,2},{4,5},{5,4},{6,7},{7,6},{8,9},{9,8},{10,11... | collective-permute-start | bytes 294920 | tf_op jit(solution)/shard_map/ppermute | solution.py:202
  31.3 4.5 %collective-permute-start.2 = (bf16[1,3,16,1024]{3,2,1,0:T(8,128)(2,1)S(1)}, bf16[1,3,16,1024]{3,2,1,0:T(8,128)(2,1)S(1)}, u32[]{:S(2)}, u32[]{:S(2)}) collective-permute-start(bf16[1,3,16,1024]{3,2,1,0:T(8,128)(2,1)S(1)} %shard_map.48.refs_0_), channel_id=1, source_target_pairs={{0,192},{32,224},{64,0},{96,32},{128,64},{160,96},{192,128},{224,1... | collective-permute-start | bytes 294920 | tf_op jit(solution)/shard_map/ppermute | solution.py:206
  32.0 6.1 %collective-permute-start.1 = (bf16[1,3,16,1024]{3,2,1,0:T(8,128)(2,1)S(1)}, bf16[1,3,16,1024]{3,2,1,0:T(8,128)(2,1)S(1)}, u32[]{:S(2)}, u32[]{:S(2)}) collective-permute-start(bf16[1,3,16,1024]{3,2,1,0:T(8,128)(2,1)S(1)} %shard_map.48.refs_0_), channel_id=1, source_target_pairs={{0,64},{32,96},{64,128},{96,160},{128,192},{160,224},{192,0},{224,... | collective-permute-start | bytes 294920 | tf_op jit(solution)/shard_map/ppermute | solution.py:206
  33.7 7.7 %collective-permute-start.3 = (bf16[1,3,16,1024]{3,2,1,0:T(8,128)(2,1)S(1)}, bf16[1,3,16,1024]{3,2,1,0:T(8,128)(2,1)S(1)}, u32[]{:S(2)}, u32[]{:S(2)}) collective-permute-start(bf16[1,3,16,1024]{3,2,1,0:T(8,128)(2,1)S(1)} %shard_map.48.refs_0_), channel_id=1, source_target_pairs={{0,128},{32,160},{64,192},{96,224},{128,0},{160,32},{192,64},{224,... | collective-permute-start | bytes 294920 | tf_op jit(solution)/shard_map/ppermute | solution.py:206
  35.8 15.0 %collective-permute-start.7 = (bf16[3,3,16,1024]{3,2,1,0:T(8,128)(2,1)S(1)}, bf16[3,3,16,1024]{3,2,1,0:T(8,128)(2,1)S(1)}, u32[]{:S(2)}, u32[]{:S(2)}) collective-permute-start(bf16[3,3,16,1024]{3,2,1,0:T(8,128)(2,1)S(1)} %shard_map.53), channel_id=1, source_target_pairs={{0,224},{32,0},{64,32},{96,64},{128,96},{160,128},{192,160},{224,1... | collective-permute-start | bytes 884744 | tf_op jit(solution)/shard_map/ppermute | solution.py:206
  38.2 12.7 %collective-permute-start.6 = (bf16[3,3,16,1024]{3,2,1,0:T(8,128)(2,1)S(1)}, bf16[3,3,16,1024]{3,2,1,0:T(8,128)(2,1)S(1)}, u32[]{:S(2)}, u32[]{:S(2)}) collective-permute-start(bf16[3,3,16,1024]{3,2,1,0:T(8,128)(2,1)S(1)} %shard_map.52), channel_id=1, source_target_pairs={{0,32},{32,64},{64,96},{96,128},{128,160},{160,192},{192,224},{224... | collective-permute-start | bytes 884744 | tf_op jit(solution)/shard_map/ppermute | solution.py:206
  41.5 9.4 %collective-permute-start.5 = (bf16[3,3,16,1024]{3,2,1,0:T(8,128)(2,1)S(1)}, bf16[3,3,16,1024]{3,2,1,0:T(8,128)(2,1)S(1)}, u32[]{:S(2)}, u32[]{:S(2)}) collective-permute-start(bf16[3,3,16,1024]{3,2,1,0:T(8,128)(2,1)S(1)} %shard_map.51.after_ref), channel_id=1, source_target_pairs={{0,1},{1,0},{2,3},{3,2},{4,5},{5,4},{6,7},{7,6},{8,9},{9,8},{10,11... | collective-permute-start | bytes 884744 | tf_op jit(solution)/shard_map/ppermute | solution.py:202
  41.7 9.1 %collective-permute-start.8 = (bf16[2,3,16,1024]{3,2,1,0:T(8,128)(2,1)S(1)}, bf16[2,3,16,1024]{3,2,1,0:T(8,128)(2,1)S(1)}, u32[]{:S(2)}, u32[]{:S(2)}) collective-permute-start(bf16[2,3,16,1024]{3,2,1,0:T(8,128)(2,1)S(1)} %shard_map.49.head), channel_id=1, source_target_pairs={{0,16},{16,0},{1,17},{17,1},{2,18},{18,2},{3,19},{19,3},{4,20},{20... | collective-permute-start | bytes 589832 | tf_op jit(solution)/shard_map/ppermute | solution.py:202
  50.9 6.2 %collective-permute-start.9 = (bf16[12,3,16,1024]{3,2,1,0:T(8,128)(2,1)S(1)}, bf16[12,3,16,1024]{3,2,1,0:T(8,128)(2,1)S(1)}, u32[]{:S(2)}, u32[]{:S(2)}) collective-permute-start(bf16[12,3,16,1024]{3,2,1,0:T(8,128)(2,1)S(1)} %shard_map.55.middle), channel_id=1, source_target_pairs={{0,16},{16,0},{1,17},{17,1},{2,18},{18,2},{3,19},{19,3},{4,20},{20... | collective-permute-start | bytes 3538952 | tf_op jit(solution)/shard_map/ppermute | solution.py:202
  54.3 5.7 %collective-permute-start.10 = (bf16[1,3,16,1024]{3,2,1,0:T(8,128)(2,1)S(1)}, bf16[1,3,16,1024]{3,2,1,0:T(8,128)(2,1)S(1)}, u32[]{:S(2)}, u32[]{:S(2)}) collective-permute-start(bf16[1,3,16,1024]{3,2,1,0:T(8,128)(2,1)S(1)} %get-tuple-element.36), channel_id=1, source_target_pairs={{0,32},{32,64},{64,96},{96,128},{128,160},{160,192},{192,224},{224... | collective-permute-start | bytes 294920 | tf_op jit(solution)/shard_map/ppermute | solution.py:206
  54.4 5.6 %collective-permute-start.11 = (bf16[1,3,16,1024]{3,2,1,0:T(8,128)(2,1)S(1)}, bf16[1,3,16,1024]{3,2,1,0:T(8,128)(2,1)S(1)}, u32[]{:S(2)}, u32[]{:S(2)}) collective-permute-start(bf16[1,3,16,1024]{3,2,1,0:T(8,128)(2,1)S(1)} %get-tuple-element.37), channel_id=1, source_target_pairs={{0,224},{32,0},{64,32},{96,64},{128,96},{160,128},{192,160},{224,1... | collective-permute-start | bytes 294920 | tf_op jit(solution)/shard_map/ppermute | solution.py:206
  60.1 2.0 %collective-permute-start.12 = (bf16[2,3,16,1024]{3,2,1,0:T(8,128)(2,1)S(1)}, bf16[2,3,16,1024]{3,2,1,0:T(8,128)(2,1)S(1)}, u32[]{:S(2)}, u32[]{:S(2)}) collective-permute-start(bf16[2,3,16,1024]{3,2,1,0:T(8,128)(2,1)S(1)} %shard_map.58.last), channel_id=1, source_target_pairs={{0,16},{16,0},{1,17},{17,1},{2,18},{18,2},{3,19},{19,3},{4,20},{20... | collective-permute-start | bytes 589832 | tf_op jit(solution)/shard_map/ppermute | solution.py:202
